TPU v7x, 256 devices: a whole 4x4x8 slice. The times are simulated.
256 devices in a mesh: leaf: 256 (over y, x, z, core).
Axes of the slice: x: 4, y: 4, z: 8, core: 2. Of those that a mesh axis runs over, the one named last changes fastest.
Arguments:
- features: float32 [8, 1048576], P(None, 'leaf'), as said below
- solution: float32 [64, 1048576], P(None, 'leaf'), may hold values from -6 to 6
- residual: float32 [64, 1048576], P(None, 'leaf')
- direction: float32 [64, 1048576], P(None, 'leaf')
- neighbours: int32 [4096, 8], P('leaf'), may hold values from -1 to 4095, as said below
- skeleton_basis: float32 [128, 1048576], P(None, 'leaf'), may hold values from -0.09375 to 0.09375
- base_skeleton: int32 [256, 128], P('leaf'), may hold values from 0 to 4095, as said below
- upper_skeleton: int32 [256, 8, 128], P('leaf'), may hold values from 0 to 255, as said below
- transfer: float32 [256, 8, 256, 128], P('leaf'), as said below
Outputs:
- new_solution: float32 [64, 1048576], P(None, 'leaf')
- new_residual: float32 [64, 1048576], P(None, 'leaf')
- new_direction: float32 [64, 1048576], P(None, 'leaf')
Inputs may be any that keep to these rules, and one draw needn't show every extreme that they name: `neighbours`: row k lists the near-field partner leaves of leaf k by global leaf number, -1 for an empty slot; leaf j appears in row k exactly as often as k in row j, and no leaf lists itself. Slots 0 to 5 name leaves of the same device; on each device these slots are filled for a leading run of slots that is the same for all its leaves. Slot 6 names a leaf of the device before, slot 7 a leaf of the device after. On every device but the first exactly 4 leaves fill slot 6, and on every device but the last exactly 4 fill slot 7. No device has more than 104 filled slots, and some device has exactly that many. `base_skeleton`: each row holds 128 distinct point numbers within its device-level node. `upper_skeleton`: entry [n, l - 1] holds 128 distinct positions among the 256 skeleton points of the two children of the level-l node above node n; all nodes under one level-l node hold the same entry. `transfer`: all nodes under one level-l node hold the same matrix at [n, l - 1]. `features`: point coordinates, in tree order.
All inputs are finite; a program needn't handle non-finite values.
Results may differ from a plain program's by a relative error of at most 0.00055.
The roundings to bfloat16 on the way count: a program that leaves them out, or rounds other values in their place, can miss the bound.
Values may be sent and summed in bfloat16 or wider, within the bound.
A program may use at most 64 MiB of HBM per device.

v0:
```python
import jax
import jax.numpy as jnp
from jax import lax
from jax.sharding import PartitionSpec as P

HIGHEST = lax.Precision.HIGHEST
ridge_scale = 1.0
kernel_width = 8.0
near_weight = 0.125


def from_behind(value, axis, steps):
    count = lax.axis_size(axis)
    initial, last = (max(0, -steps), min(count, count - steps))
    return lax.ppermute(value, axis, [(source, source + steps) for source in range(initial, last)])


def from_partner(value, axis, stride):
    mask = 2**stride
    pairs = [(source, source ^ mask) for source in range(lax.axis_size(axis))]
    return lax.ppermute(value, axis, pairs)


def kernel_matrix(source, target):
    inner_prod = jnp.dot(source.T, target, precision=HIGHEST, preferred_element_type=jnp.float32)
    source_sq = jnp.sum(source * source, axis=0)
    target_sq = jnp.sum(target * target, axis=0)
    return jnp.exp(-(source_sq[:, None] + target_sq[None, :] - 2.0 * inner_prod) / kernel_width)


def kernel_tiles(source, target):
    source = source.astype(jnp.float32)
    target = target.astype(jnp.float32)
    inner_prod = jnp.einsum(
        "dnj,dni->nji", source, target, precision=HIGHEST, preferred_element_type=jnp.float32
    )
    source_sq = jnp.sum(source * source, axis=0)
    target_sq = jnp.sum(target * target, axis=0)
    return jnp.exp(
        -(source_sq[:, :, None] + target_sq[:, None, :] - 2.0 * inner_prod) / kernel_width
    ).astype(jnp.bfloat16)


def on_device(
    features,
    solution,
    residual,
    direction,
    neighbours,
    skeleton_basis,
    base_skeleton,
    upper_skeleton,
    transfer,
):
    device = lax.axis_index("leaf")
    levels = lax.axis_size("leaf").bit_length() - 1
    leaves = neighbours.shape[0]
    slots = neighbours.shape[1]
    feature_dims = features.shape[0]
    classes = direction.shape[0]
    leaf_width = features.shape[1] // leaves
    skeleton_rank = base_skeleton.shape[1]
    near_points = features.astype(jnp.bfloat16)
    near_values = direction.astype(jnp.bfloat16)
    norm_old = lax.psum(jnp.sum(residual * residual, axis=1), "leaf")
    filled = neighbours >= 0
    safe_id = jnp.where(filled, neighbours, 0)
    left_points, left_values = from_behind((near_points, near_values), "leaf", 1)
    right_points, right_values = from_behind((near_points, near_values), "leaf", -1)
    owner_dev = safe_id // leaves
    local_no = safe_id - owner_dev * leaves
    pool_spot = jnp.where(
        owner_dev == device,
        local_no,
        jnp.where(owner_dev < device, leaves + local_no, 2 * leaves + local_no),
    )
    pool_spot = jnp.where(filled, pool_spot, 0)
    pool_points = jnp.concatenate([near_points, left_points, right_points], axis=1).reshape(
        feature_dims, -1, leaf_width
    )
    pool_values = jnp.concatenate([near_values, left_values, right_values], axis=1).reshape(
        classes, -1, leaf_width
    )
    own_points = near_points.reshape(feature_dims, leaves, leaf_width)
    pool_spots = jnp.concatenate([jnp.arange(leaves)[:, None], pool_spot], axis=1)
    tile_scales = jnp.concatenate(
        [jnp.ones((leaves, 1), jnp.float32), near_weight * filled.astype(jnp.float32)], axis=1
    )

    def tile_terms(target_leaf, spot_ids, scale_row):
        tile_block = kernel_tiles(
            jnp.take(pool_points, spot_ids, axis=1), jnp.take(own_points, target_leaf, axis=1)
        )
        weighted = (
            jnp.take(pool_values, spot_ids, axis=1) * scale_row.astype(jnp.bfloat16)[None, :, None]
        )
        return (tile_block, weighted)

    def leaf_near(leaf_no):
        tile_block, weighted = tile_terms(
            jnp.full((slots + 1,), leaf_no), pool_spots[leaf_no], tile_scales[leaf_no]
        )
        return jnp.einsum("rsj,sji->ri", weighted, tile_block, preferred_element_type=jnp.float32)

    near_rows = lax.map(leaf_near, jnp.arange(leaves))
    near_field = near_rows.transpose(1, 0, 2).reshape(classes, -1)
    weights = lax.dot_general(
        skeleton_basis,
        direction,
        (((1,), (1,)), ((), ())),
        precision=HIGHEST,
        preferred_element_type=jnp.float32,
    )
    points = jnp.take(features, base_skeleton[0], axis=1)
    level_weights = [weights]
    level_points = [points]
    for level in range(levels):
        other_weights, other_points = from_partner((weights, points), "leaf", level)
        upper_half = device >> level & 1 == 1
        stacked = jnp.concatenate(
            [
                jnp.where(upper_half, other_weights, weights),
                jnp.where(upper_half, weights, other_weights),
            ],
            axis=0,
        )
        paired = jnp.concatenate(
            [
                jnp.where(upper_half, other_points, points),
                jnp.where(upper_half, points, other_points),
            ],
            axis=1,
        )
        weights = lax.dot_general(
            transfer[0, level],
            stacked,
            (((0,), (0,)), ((), ())),
            precision=HIGHEST,
            preferred_element_type=jnp.float32,
        )
        points = jnp.take(paired, upper_skeleton[0, level], axis=1)
        level_weights.append(weights)
        level_points.append(points)
    couplings = []
    for level in range(levels + 1):
        kernel_mat = kernel_matrix(level_points[level], level_points[level])
        couplings.append(
            jnp.dot(
                kernel_mat,
                level_weights[level],
                precision=HIGHEST,
                preferred_element_type=jnp.float32,
            )
        )
    descent = couplings[levels]
    for level in reversed(range(levels)):
        spread = jnp.dot(
            transfer[0, level], descent, precision=HIGHEST, preferred_element_type=jnp.float32
        )
        upper_half = device >> level & 1 == 1
        descent = couplings[level] + jnp.where(
            upper_half, spread[skeleton_rank:], spread[:skeleton_rank]
        )
    far_field = lax.dot_general(
        descent,
        skeleton_basis,
        (((0,), (0,)), ((), ())),
        precision=HIGHEST,
        preferred_element_type=jnp.float32,
    )
    image = ridge_scale * direction + near_field + far_field
    curvature = lax.psum(jnp.sum(direction * image, axis=1), "leaf")
    step_size = norm_old / curvature
    new_residual = residual - step_size[:, None] * image
    norm_new = lax.psum(jnp.sum(new_residual * new_residual, axis=1), "leaf")
    new_solution = solution + step_size[:, None] * direction
    new_direction = new_residual + (norm_new / norm_old)[:, None] * direction
    return (new_solution, new_residual, new_direction)


def solution(mesh):
    placed = (
        P(None, "leaf"),
        P(None, "leaf"),
        P(None, "leaf"),
        P(None, "leaf"),
        P("leaf", None),
        P(None, "leaf"),
        P("leaf", None),
        P("leaf", None, None),
        P("leaf", None, None, None),
    )
    return jax.shard_map(
        on_device,
        mesh=mesh,
        in_specs=placed,
        out_specs=(P(None, "leaf"), P(None, "leaf"), P(None, "leaf")),
        check_vma=False,
    )
```

profile of v0, /device:TPU:1, one launch (start us, length us, event | category | flops | bytes accessed | tf_op | source)
XLA Modules:
  0.0 500.1 jit_solution(2759324767114072106)
XLA Ops:
  1.7 4.9 collective-permute-start.2
  6.7 2.1 collective-permute-start.3
  8.8 2.1 convert_element_type.26
  10.9 3.4 collective-permute-start
  16.2 2.8 copy.59
  19.1 2.2 gather_fusion.3
  21.7 2.3 fusion.136
  36.9 5.2 %collective-permute-start.8 = (f32[8,128]{0,1:T(8,128)S(1)}, f32[8,128]{0,1:T(8,128)S(1)}, u32[]{:S(2)}, u32[]{:S(2)}) collective-permute-start(f32[8,128]{0,1:T(8,128)S(1)} %get-tuple-element.114), channel_id=1, source_target_pairs={{0,4},{1,5},{2,6},{3,7},{4,0},{5,1},{6,2},{7,3},{8,12},{9,13},{10,... | collective-permute-start | bytes 12296 | tf_op jit(solution)/shard_map/ppermute | solution.py:21
  45.3 8.5 %collective-permute-start.10 = (f32[8,128]{0,1:T(8,128)S(1)}, f32[8,128]{0,1:T(8,128)S(1)}, u32[]{:S(2)}, u32[]{:S(2)}) collective-permute-start(f32[8,128]{0,1:T(8,128)S(1)} %get-tuple-element.110), channel_id=1, source_target_pairs={{0,8},{1,9},{2,10},{3,11},{4,12},{5,13},{6,14},{7,15},{8,0},{9,1},... | collective-permute-start | bytes 12296 | tf_op jit(solution)/shard_map/ppermute | solution.py:21
  57.0 4.0 collective-permute-start.12
  63.5 3.1 collective-permute-start.14
  69.1 4.7 collective-permute-start.16
  75.4 5.5 %collective-permute-start.5 = (f32[128,64]{0,1:T(8,128)S(1)}, f32[128,64]{0,1:T(8,128)S(1)}, u32[]{:S(2)}, u32[]{:S(2)}) collective-permute-start(f32[128,64]{0,1:T(8,128)S(1)} %fusion.136), channel_id=1, source_target_pairs={{0,1},{1,0},{2,3},{3,2},{4,5},{5,4},{6,7},{7,6},{8,9},{9,8},{10,11... | collective-permute-start | bytes 98312 | tf_op jit(solution)/shard_map/ppermute | solution.py:21
  88.3 3.1 collective-permute-done.9
  91.4 3.4 collective-permute-start.18
  96.5 6.7 %collective-permute-done.11 = f32[128,64]{0,1:T(8,128)S(1)} collective-permute-done((f32[128,64]{0,1:T(8,128)S(1)}, f32[128,64]{0,1:T(8,128)S(1)}, u32[]{:S(2)}, u32[]{:S(2)}) %collective-permute-start.11) | collective-permute-done | bytes 32800 | tf_op jit(solution)/shard_map/ppermute | solution.py:21
  109.2 3.4 collective-permute-done.15
  117.8 3.1 collective-permute-start.19
  134.8 200.1 %while.10 = (s32[]{:T(128)}, f32[16,64,256]{2,1,0:T(8,128)}, s32[16]{0:T(128)}, s32[16,9]{1,0:T(8,128)S(1)}, bf16[64,48,256]{2,0,1:T(8,128)(2,1)}, /*index=5*/bf...) while((s32[]{:T(128)}, f32[16,64,256]{2,1,0:T(8,128)}, ...), condition=%wide.region_5.6_spmd, body=%wide.region_2.5_spmd.sunk | while | flops 88950360 | bytes 3650664 | solution.py:105
  142.3 2.0 gather_fusion.2
  145.0 2.3 fusion.196
  157.5 2.3 fusion.196
  167.3 2.0 gather_fusion.2
  170.0 2.3 fusion.196
  182.5 2.3 fusion.196
  195.0 2.3 fusion.196
  204.9 2.0 gather_fusion.2
  207.5 2.3 fusion.196
  217.4 2.0 gather_fusion.2
  220.0 2.3 fusion.196
  229.9 2.0 gather_fusion.2
  232.6 2.3 fusion.196
  242.4 2.0 gather_fusion.2
  245.1 2.3 fusion.196
  257.6 2.3 fusion.196
  270.1 2.3 fusion.196
  279.9 2.0 gather_fusion.2
  282.6 2.3 fusion.196
  292.4 2.0 gather_fusion.2
  295.1 2.3 fusion.196
  307.6 2.3 fusion.196
  320.1 2.3 fusion.196
  332.6 2.3 fusion.196
  336.2 2.5 multiply_reduce_fusion.3
  338.7 82.1 %all-reduce.1 = (f32[64]{0:T(128)S(1)}, f32[64]{0:T(128)S(1)}) all-reduce(f32[64]{0:T(128)S(1)} %copy-done.11, f32[64]{0:T(128)S(1)} %get-tuple-element.173), channel_id=1, replica_groups=mesh['leaf'=256] {'leaf'}, use_global_device_ids=true, to_apply=%region_1.0 | all-reduce | flops 128 | bytes 1024 | tf_op jit(solution)/shard_map/psum | solution.py:65
  420.8 2.8 multiply_reduce_fusion.2
  423.6 73.3 %psum.23 = f32[64]{0:T(128)S(1)} all-reduce(f32[64]{0:T(128)S(1)} %get-tuple-element.89), channel_id=1, replica_groups=mesh['leaf'=256] {'leaf'}, use_global_device_ids=true, to_apply=%region_18.20 | all-reduce | flops 64 | bytes 512 | tf_op jit(solution)/shard_map/psum | solution.py:175
  497.0 3.1 multiply_add_fusion
  (339 shorter events, 178.0 us)
Async XLA Ops:
  0.6 21.0 %copy-start = (f32[128,4096]{1,0:T(8,128)S(1)}, f32[128,4096]{1,0:T(8,128)}, u32[]{:S(2)}) copy-start(f32[128,4096]{1,0:T(8,128)} %param.18) | copy-start | bytes 6291460
  0.6 21.0 %copy-start.1 = (f32[64,4096]{1,0:T(8,128)S(1)}, f32[64,4096]{1,0:T(8,128)}, u32[]{:S(2)}) copy-start(f32[64,4096]{1,0:T(8,128)} %param.16) | copy-start | bytes 3145732
  0.7 18.4 %copy-start.12 = (s32[1,128]{1,0:T(1,128)S(1)}, s32[1,128]{1,0:T(1,128)}, u32[]{:S(2)}) copy-start(s32[1,128]{1,0:T(1,128)} %param.19) | copy-start | bytes 1540
  1.7 119.1 %collective-permute-start.2 = (bf16[8,4096]{1,0:T(8,128)(2,1)S(1)}, bf16[8,4096]{1,0:T(8,128)(2,1)}, u32[]{:S(2)}, u32[]{:S(2)}) collective-permute-start(bf16[8,4096]{1,0:T(8,128)(2,1)S(1)} %convert_element_type.27), channel_id=1, source_target_pairs={{0,1},{1,2},{2,3},{3,4},{4,5},{5,6},{6,7},{7,8},{8,9},{9,10},{10,1... | collective-permute-start | bytes 196616 | tf_op jit(solution)/shard_map/ppermute | solution.py:15
  6.7 114.2 %collective-permute-start.3 = (bf16[8,4096]{1,0:T(8,128)(2,1)S(1)}, bf16[8,4096]{1,0:T(8,128)(2,1)}, u32[]{:S(2)}, u32[]{:S(2)}) collective-permute-start(bf16[8,4096]{1,0:T(8,128)(2,1)S(1)} %convert_element_type.27), channel_id=1, source_target_pairs={{1,0},{2,1},{3,2},{4,3},{5,4},{6,5},{7,6},{8,7},{9,8},{10,9},{11,1... | collective-permute-start | bytes 196616 | tf_op jit(solution)/shard_map/ppermute | solution.py:15
  10.9 120.5 %collective-permute-start = (bf16[64,4096]{1,0:T(8,128)(2,1)}, bf16[64,4096]{1,0:T(8,128)(2,1)}, u32[]{:S(2)}, u32[]{:S(2)}) collective-permute-start(bf16[64,4096]{1,0:T(8,128)(2,1)} %convert_element_type.26), channel_id=1, source_target_pairs={{0,1},{1,2},{2,3},{3,4},{4,5},{5,6},{6,7},{7,8},{8,9},{9,10},{10,1... | collective-permute-start | bytes 1572872 | tf_op jit(solution)/shard_map/ppermute | solution.py:15
  14.3 117.1 %collective-permute-start.1 = (bf16[64,4096]{1,0:T(8,128)(2,1)}, bf16[64,4096]{1,0:T(8,128)(2,1)}, u32[]{:S(2)}, u32[]{:S(2)}) collective-permute-start(bf16[64,4096]{1,0:T(8,128)(2,1)} %convert_element_type.26), channel_id=1, source_target_pairs={{1,0},{2,1},{3,2},{4,3},{5,4},{6,5},{7,6},{8,7},{9,8},{10,9},{11,1... | collective-permute-start | bytes 1572872 | tf_op jit(solution)/shard_map/ppermute | solution.py:15
  19.1 4.8 copy-start.8
  19.1 6.5 %copy-start.9 = (s32[16,8]{0,1:T(8,128)S(1)}, s32[16,8]{0,1:T(8,128)}, u32[]{:S(2)}) copy-start(s32[16,8]{0,1:T(8,128)} %param.17) | copy-start | bytes 1540
  21.5 6.8 %collective-permute-start.4 = (f32[8,128]{0,1:T(8,128)S(1)}, f32[8,128]{0,1:T(8,128)S(1)}, u32[]{:S(2)}, u32[]{:S(2)}) collective-permute-start(f32[8,128]{0,1:T(8,128)S(1)} %get-tuple-element.122), channel_id=1, source_target_pairs={{0,1},{1,0},{2,3},{3,2},{4,5},{5,4},{6,7},{7,6},{8,9},{9,8},{10,11... | collective-permute-start | bytes 12296 | tf_op jit(solution)/shard_map/ppermute | solution.py:21
  27.7 35.6 %copy-start.10 = (pred[128]{0:T(512)(128)(4,1)S(1)}, pred[128]{0:T(512)(128)(4,1)}, u32[]{:S(2)}) copy-start(pred[128]{0:T(512)(128)(4,1)} %get-tuple-element.161) | copy-start | bytes 388
  31.4 4.0 collective-permute-start.6
  36.9 6.9 %collective-permute-start.8 = (f32[8,128]{0,1:T(8,128)S(1)}, f32[8,128]{0,1:T(8,128)S(1)}, u32[]{:S(2)}, u32[]{:S(2)}) collective-permute-start(f32[8,128]{0,1:T(8,128)S(1)} %get-tuple-element.114), channel_id=1, source_target_pairs={{0,4},{1,5},{2,6},{3,7},{4,0},{5,1},{6,2},{7,3},{8,12},{9,13},{10,... | collective-permute-start | bytes 12296 | tf_op jit(solution)/shard_map/ppermute | solution.py:21
  45.3 10.2 %collective-permute-start.10 = (f32[8,128]{0,1:T(8,128)S(1)}, f32[8,128]{0,1:T(8,128)S(1)}, u32[]{:S(2)}, u32[]{:S(2)}) collective-permute-start(f32[8,128]{0,1:T(8,128)S(1)} %get-tuple-element.110), channel_id=1, source_target_pairs={{0,8},{1,9},{2,10},{3,11},{4,12},{5,13},{6,14},{7,15},{8,0},{9,1},... | collective-permute-start | bytes 12296 | tf_op jit(solution)/shard_map/ppermute | solution.py:21
  57.0 5.6 %collective-permute-start.12 = (f32[8,128]{0,1:T(8,128)S(1)}, f32[8,128]{0,1:T(8,128)S(1)}, u32[]{:S(2)}, u32[]{:S(2)}) collective-permute-start(f32[8,128]{0,1:T(8,128)S(1)} %get-tuple-element.106), channel_id=1, source_target_pairs={{0,16},{1,17},{2,18},{3,19},{4,20},{5,21},{6,22},{7,23},{8,24},{9,... | collective-permute-start | bytes 12296 | tf_op jit(solution)/shard_map/ppermute | solution.py:21
  63.5 4.7 collective-permute-start.14
  69.1 6.4 %collective-permute-start.16 = (f32[8,128]{0,1:T(8,128)S(1)}, f32[8,128]{0,1:T(8,128)S(1)}, u32[]{:S(2)}, u32[]{:S(2)}) collective-permute-start(f32[8,128]{0,1:T(8,128)S(1)} %get-tuple-element.98), channel_id=1, source_target_pairs={{0,64},{1,65},{2,66},{3,67},{4,68},{5,69},{6,70},{7,71},{8,72},{9,... | collective-permute-start | bytes 12296 | tf_op jit(solution)/shard_map/ppermute | solution.py:21
  75.4 6.8 %collective-permute-start.5 = (f32[128,64]{0,1:T(8,128)S(1)}, f32[128,64]{0,1:T(8,128)S(1)}, u32[]{:S(2)}, u32[]{:S(2)}) collective-permute-start(f32[128,64]{0,1:T(8,128)S(1)} %fusion.136), channel_id=1, source_target_pairs={{0,1},{1,0},{2,3},{3,2},{4,5},{5,4},{6,7},{7,6},{8,9},{9,8},{10,11... | collective-permute-start | bytes 98312 | tf_op jit(solution)/shard_map/ppermute | solution.py:21
  83.3 2.9 collective-permute-start.7
  87.3 4.1 collective-permute-start.9
  91.4 5.0 %collective-permute-start.18 = (f32[8,128]{0,1:T(8,128)S(1)}, f32[8,128]{0,1:T(8,128)S(1)}, u32[]{:S(2)}, u32[]{:S(2)}) collective-permute-start(f32[8,128]{0,1:T(8,128)S(1)} %get-tuple-element.94), channel_id=1, source_target_pairs={{0,128},{1,129},{2,130},{3,131},{4,132},{5,133},{6,134},{7,135},{8... | collective-permute-start | bytes 12296 | tf_op jit(solution)/shard_map/ppermute | solution.py:21
  96.4 6.7 %collective-permute-start.11 = (f32[128,64]{0,1:T(8,128)S(1)}, f32[128,64]{0,1:T(8,128)S(1)}, u32[]{:S(2)}, u32[]{:S(2)}) collective-permute-start(f32[128,64]{0,1:T(8,128)S(1)} %bitcast.245), channel_id=1, source_target_pairs={{0,8},{1,9},{2,10},{3,11},{4,12},{5,13},{6,14},{7,15},{8,0},{9,1},... | collective-permute-start | bytes 98312 | tf_op jit(solution)/shard_map/ppermute | solution.py:21
  104.3 2.9 collective-permute-start.13
  106.6 2.6 copy-start.6
  106.6 17.3 %copy-start.2 = (f32[1,8,256,128]{3,2,1,0:T(8,128)S(1)}, f32[1,8,256,128]{3,2,1,0:T(8,128)}, u32[]{:S(2)}) copy-start(f32[1,8,256,128]{3,2,1,0:T(8,128)} %param.21) | copy-start | bytes 3145732
  106.6 17.5 %copy-start.5 = (f32[128,128]{1,0:T(8,128)S(1)}, f32[128,128]{1,0:T(8,128)}, u32[]{:S(2)}) copy-start(f32[128,128]{1,0:T(8,128)} %fusion.22) | copy-start | bytes 196612
  107.1 23.0 %copy-start.4 = (f32[128,128]{1,0:T(8,128)S(1)}, f32[128,128]{1,0:T(8,128)}, u32[]{:S(2)}) copy-start(f32[128,128]{1,0:T(8,128)} %fusion.42) | copy-start | bytes 196612
  108.3 4.4 collective-permute-start.15
  112.7 17.9 %copy-start.3 = (f32[128,128]{1,0:T(8,128)S(1)}, f32[128,128]{1,0:T(8,128)}, u32[]{:S(2)}) copy-start(f32[128,128]{1,0:T(8,128)} %fusion.46) | copy-start | bytes 196612
  113.8 2.9 collective-permute-start.17
  116.5 14.6 %copy-start.7 = (f32[128,128]{1,0:T(8,128)S(1)}, f32[128,128]{1,0:T(8,128)}, u32[]{:S(2)}) copy-start(f32[128,128]{1,0:T(8,128)} %fusion.50) | copy-start | bytes 196612
  117.8 4.6 collective-permute-start.19
  336.2 2.5 copy-start.11
where the time goes:
time: 504 us; the launch traced here: 500 us
  blocking collectives  155 us (31%)
  local copies, waits for them, and re-layouts  113 us (22%)
  matrix products  97.4 us (19%)
  starting transfers between devices  53.6 us (11%)
  loops' own time  34.3 us (7%)
  other arithmetic  24.2 us (5%)
  waiting for transfers between devices  21.2 us (4%)
    psum x1, blocking collectives, on_device(): norm_old = lax.psum(jnp.sum(residual * residual, axis=1), 'leaf')  82.1 us
    psum x1, blocking collectives, on_device(): norm_new = lax.psum(jnp.sum(new_residual * new_residual, axis=1), 'leaf')  73.3 us
    ppermute x16, starting transfers between devices, from_partner(): return lax.ppermute(value, axis, pairs)  41.2 us
    dot_general x16, matrix products, leaf_near(): jnp.einsum('rsj,sji->ri', weighted, tile_block, preferred_element_type=jn...  36.4 us
    another operation x1, loops' own time, on_device(): near_rows = lax.map(leaf_near, jnp.arange(leaves))  34.3 us
    gather x16, local copies, waits for them, and re-layouts, tile_terms(): jnp.take(pool_values, spot_ids, axis=1)  31.5 us
    dot_general x16, matrix products, kernel_tiles(): jnp.einsum('dnj,dni->nji', source, target, precision=HIGHEST, preferred_e...  30.9 us
    gather x16, local copies, waits for them, and re-layouts, tile_terms(): jnp.take(pool_points, spot_ids, axis=1)  23.7 us
  transfers between devices with their start and end apart: 20, of which 13 were waited for; matrix products, arithmetic and copies ran while one was open for 11% of the time, Pallas kernels for 0%

commit v1 on v0

v1 whole, which is shorter than its diff:
```python
import functools

import jax
import jax.numpy as jnp
from jax import lax
from jax.experimental import pallas as pl
from jax.experimental.pallas import tpu as pltpu
from jax.sharding import PartitionSpec as P

f32 = jnp.float32
bf16 = jnp.bfloat16
MESH = pl.DeviceIdType.MESH
NN = (((1,), (0,)), ((), ()))
NT = (((1,), (1,)), ((), ()))

LEVELS = 8
GROUP = 16
LEAVES = 16
WIDTH = 256
INNER = 6
BOUND = 4
RANK = 128
CLASSES = 64
DIMS = 8
CHUNK = 512
MASKS = (1, 2, 4, 14, 16, 48, 64, 192)
SHARE = (0, 2, 4, 4, 3, 3, 0, 0)


def flip(me, mask):
    out = me
    for bit in range(LEVELS):
        if mask >> bit & 1:
            out = out + (1 - 2 * (me // 2**bit % 2)) * 2**bit
    return out


def dot(a, b, dims=NN):
    return lax.dot_general(a, b, dims, preferred_element_type=f32)


def split2(x):
    high = x.astype(bf16)
    return high, (x - high.astype(f32)).astype(bf16)


def split3(x):
    high = x.astype(bf16).astype(f32)
    rest = x - high
    mid = rest.astype(bf16).astype(f32)
    return high, mid, (rest - mid).astype(bf16).astype(f32)


def dot3(a, b, dims=NN):
    (ah, al), (bh, bl) = a, b
    rows = ah.shape[0]
    both = dot(jnp.concatenate([ah, al], axis=0), bh, dims)
    return both[:rows] + both[rows:] + dot(ah, bl, dims)


def norm_rows(norm, scale, swapped):
    high, mid, low = split3(norm)
    shape = (8, norm.shape[1])
    row = lax.broadcasted_iota(jnp.int32, shape, 0)
    first = 3 if swapped else 0
    ones = 0 if swapped else 3
    out = jnp.where((row >= ones) & (row < ones + 3), 1.0, 0.0).astype(f32)
    for i, piece in enumerate((high, mid, low)):
        out = jnp.where(row == first + i, jnp.broadcast_to(piece, shape), out)
    return out * scale


def gaussian(points):
    h, m, l = split3(points)
    norm = jnp.sum(points * points, axis=0, keepdims=True)
    pad = jnp.zeros_like(points)
    left = jnp.concatenate([h, h, m, h, m, l, norm_rows(norm, 1.0, False), pad], axis=0)
    right = jnp.concatenate(
        [0.25 * h, 0.25 * m, 0.25 * h, 0.25 * l, 0.25 * m, 0.25 * h, norm_rows(norm, -0.125, True), pad],
        axis=0,
    )
    return jnp.exp(dot(left.T.astype(bf16), right.astype(bf16)))


def pick(points, chosen):
    h, m, l = split3(points)
    stack = jnp.concatenate([h, m, l, jnp.zeros_like(h)], axis=0).astype(bf16)
    out = dot(stack, chosen)
    return (out[0:8] + out[8:16]) + out[16:24]


def one_hot(index_row, start, rows):
    at = lax.broadcasted_iota(jnp.int32, (rows, index_row.shape[1]), 0) + start
    return jnp.where(at == index_row, 1.0, 0.0).astype(bf16)


def kernel(
    nbr, base_ref, upper_ref, feat_ref, dir_any, res_any, basis_any, trans_any,
    nr_ref, ab_ref,
    dir_v, res_v, basis_v, trans_v, basis_h, basis_l, trans_h, trans_l, hots,
    source_v, target_v, value_v, near_v, edge_v, pos_s,
    tree_out, tree_in, halo_out, halo_in, lo_out, lo_in, hi_out, hi_in,
    local_sem, tree_s, tree_r, halo_s, halo_r, lo_s, lo_r, hi_s, hi_r,
):
    me = lax.axis_index("leaf")
    lo_id = me % GROUP
    hi_id = me // GROUP
    halves = [me // 2**level % 2 for level in range(LEVELS)]

    copies = {}
    quarter = basis_v.shape[1] // 4
    copies["dir"] = pltpu.make_async_copy(dir_any, dir_v, local_sem.at[0])
    copies["dir"].start()
    for i in range(4):
        cols = pl.ds(i * quarter, quarter)
        copies[i] = pltpu.make_async_copy(basis_any.at[:, cols], basis_v.at[:, cols], local_sem.at[1 + i])
        copies[i].start()
    copies["trans"] = pltpu.make_async_copy(trans_any.at[0], trans_v, local_sem.at[5])
    copies["trans"].start()
    copies["res"] = pltpu.make_async_copy(res_any, res_v, local_sem.at[6])
    copies["res"].start()

    barrier = pltpu.get_barrier_semaphore()
    right = (me + 1) % 256
    left = (me + 255) % 256
    peers = [right, left]
    peers += [hi_id * GROUP + (lo_id + m) % GROUP for m in range(1, GROUP)]
    peers += [(me + GROUP * m) % 256 for m in range(1, GROUP)]
    for peer in peers:
        pl.semaphore_signal(barrier, inc=1, device_id=(peer,), device_id_type=MESH)

    edges = []
    for slot in (6, 7):
        count = jnp.int32(0)
        mine = [jnp.int32(0)] * BOUND
        theirs = [jnp.int32(0)] * BOUND
        for k in range(LEAVES):
            partner = nbr[k, slot]
            filled = partner >= 0
            place = jnp.minimum(count, BOUND - 1) + (BOUND + 1 if slot == 6 else 0)
            pos_s[slot - 6, k] = jnp.where(filled, place, BOUND)
            for q in range(BOUND):
                here = filled & (count == q)
                mine[q] = jnp.where(here, k, mine[q])
                theirs[q] = jnp.where(here, partner, theirs[q])
            count = count + filled.astype(jnp.int32)
        ranks = []
        for q in range(BOUND):
            rank = jnp.int32(0)
            for p in range(BOUND):
                if p != q:
                    rank = rank + (theirs[p] < theirs[q]).astype(jnp.int32)
            ranks.append(jnp.minimum(rank, BOUND - 1))
        edges.append((mine, ranks))

    points = jnp.zeros((32, RANK), f32)
    base_row = base_ref[...]
    for c in range(feat_ref.shape[1] // CHUNK):
        feat = feat_ref[:, c * CHUNK : (c + 1) * CHUNK]
        h, m, l = split3(feat)
        stack = jnp.concatenate([h, m, l, jnp.zeros_like(h)], axis=0).astype(bf16)
        points = points + dot(stack, one_hot(base_row, c * CHUNK, CHUNK))
        norm = jnp.sum(h * h, axis=0, keepdims=True)
        source = jnp.concatenate([h, norm_rows(norm, 1.0, False)], axis=0)
        target = jnp.concatenate([0.25 * h, norm_rows(norm, -0.125, True)], axis=0)
        for i in range(CHUNK // WIDTH):
            k = c * (CHUNK // WIDTH) + i
            block = source[:, i * WIDTH : (i + 1) * WIDTH]
            value_v[k, CLASSES:, :] = block.astype(bf16)
            source_v[k] = block.T.astype(bf16)
            target_v[k] = target[:, i * WIDTH : (i + 1) * WIDTH].astype(bf16)
    points = (points[0:8] + points[8:16]) + points[16:24]

    copies["dir"].wait()
    weights = jnp.zeros((CLASSES, RANK), f32)
    for c in range(dir_v.shape[1] // CHUNK):
        if c % (quarter // CHUNK) == 0:
            copies[c // (quarter // CHUNK)].wait()
        cols = slice(c * CHUNK, (c + 1) * CHUNK)
        dh, dl = split2(dir_v[:, cols])
        bh, bl = split2(basis_v[:, cols])
        basis_h[:, cols] = bh
        basis_l[:, cols] = bl
        for i in range(CHUNK // WIDTH):
            value_v[c * (CHUNK // WIDTH) + i, :CLASSES, :] = dh[:, i * WIDTH : (i + 1) * WIDTH]
        weights = weights + dot3((dh, dl), (bh, bl), NT)

    pl.semaphore_wait(barrier, len(peers))

    def tile(source, k):
        return jnp.exp(dot(source, target_v[k])).astype(bf16)

    def near_leaf(k, carry):
        own = dot(value_v[k, :CLASSES, :], tile(source_v[k], k))
        sides = jnp.zeros((CLASSES, WIDTH), f32)
        for s in range(INNER):
            partner = nbr[k, s]
            filled = partner >= 0
            j = jnp.clip(partner - me * LEAVES, 0, LEAVES - 1)
            scale = jnp.where(filled, 0.125, 0.0).astype(f32)
            sides = sides + scale * dot(value_v[j, :CLASSES, :], tile(source_v[j], k))
        near_v[k] = own + sides
        return carry

    def near_edge(side, at):
        mine, ranks = edges[side]
        for q in range(BOUND):
            block = halo_in[side, ranks[q]]
            source = block[CLASSES:].astype(f32).T.astype(bf16)
            edge_v[at + q] = 0.125 * dot(block[:CLASSES], tile(source, mine[q]))

    def lane_sums(x):
        out = x[:, :RANK]
        for i in range(1, x.shape[1] // RANK):
            out = out + x[:, i * RANK : (i + 1) * RANK]
        return out

    def as_row(top, bottom):
        return jnp.sum(jnp.concatenate([top, bottom], axis=0).T, axis=0, keepdims=True)

    def as_columns(row):
        return jnp.broadcast_to(row, (RANK, RANK)).T

    def spread(row, out, into, sems, recvs, use, own_id, where):
        out[use] = row
        into[use, own_id] = row
        started = []
        for m in range(1, GROUP):
            peer, slot = where(m)
            send = pltpu.make_async_remote_copy(
                src_ref=out.at[use], dst_ref=into.at[use, own_id],
                send_sem=sems.at[use, m], recv_sem=recvs.at[use, own_id],
                device_id=(peer,), device_id_type=MESH,
            )
            send.start()
            arrival = pltpu.make_async_remote_copy(
                src_ref=out.at[use], dst_ref=into.at[use, slot],
                send_sem=sems.at[use, m], recv_sem=recvs.at[use, slot],
                device_id=(peer,), device_id_type=MESH,
            )
            started.append((send, arrival))
        return started

    def lo_peer(m):
        slot = (lo_id + m) % GROUP
        return hi_id * GROUP + slot, slot

    def hi_peer(m):
        slot = (hi_id + m) % GROUP
        return slot * GROUP + lo_id, slot

    def total(started, into, use):
        for _, arrival in started:
            arrival.wait_recv()
        return jnp.sum(into[use], axis=0)

    sent = []
    lo_first = hi_first = None
    halo_copies = []
    done = 0
    matrix = None
    descent = None
    quad = jnp.zeros((CLASSES, RANK), f32)
    group_quad = jnp.zeros((CLASSES, RANK), f32)
    for level in range(LEVELS):
        tree_out[level, :CLASSES] = weights
        tree_out[level, CLASSES:] = points
        message = pltpu.make_async_remote_copy(
            src_ref=tree_out.at[level], dst_ref=tree_in.at[level],
            send_sem=tree_s.at[level], recv_sem=tree_r.at[level],
            device_id=(flip(me, MASKS[level]),), device_id_type=MESH,
        )
        message.start()
        sent.append(message)
        if level == 0:
            copies["trans"].wait()
            for i in range(LEVELS):
                th, tl = split2(trans_v[i])
                trans_h[i] = th
                trans_l[i] = tl
                hots[i] = one_hot(upper_ref[0, i : i + 1, :], 0, 2 * RANK)
        half = halves[level]
        mine = pl.ds(pl.multiple_of(half * RANK, RANK), RANK)
        other = pl.ds(pl.multiple_of((1 - half) * RANK, RANK), RANK)
        step = (trans_h[level, mine], trans_l[level, mine])
        part = dot3(split2(weights), step)
        if level == 0:
            for side, target in ((0, left), (1, right)):
                leaves = edges[side][0]
                for q in range(BOUND):
                    halo_out[side, q] = value_v[leaves[q]]
                halo = pltpu.make_async_remote_copy(
                    src_ref=halo_out.at[side], dst_ref=halo_in.at[1 - side],
                    send_sem=halo_s.at[side], recv_sem=halo_r.at[1 - side],
                    device_id=(target,), device_id_type=MESH,
                )
                halo.start()
                halo_copies.append(halo)
        couple = dot3(split2(weights), split2(gaussian(points)))
        if level == 0:
            descent = couple
        else:
            descent = descent + dot3(split2(couple), matrix, NT)
        if level < 4:
            quad = quad + 0.5**level * (weights * couple)
        else:
            group_quad = group_quad + 0.5 ** (level - 4) * (weights * couple)
        if level == 0:
            matrix = step
        else:
            matrix = split2(dot3(matrix, step))
        if SHARE[level]:
            lax.fori_loop(done, done + SHARE[level], near_leaf, 0)
            done += SHARE[level]
        if level == 3:
            halo_copies[0].wait_recv()
            halo_copies[1].wait_recv()
            edge_v[4] = jnp.zeros((CLASSES, WIDTH), f32)
            near_edge(1, 0)
            near_edge(0, 5)
        if level == 6:
            copies["res"].wait()

            def finish_leaf(k, carry):
                curve, norm = carry
                cols = pl.ds(pl.multiple_of(k * WIDTH, WIDTH), WIDTH)
                d = dir_v[:, cols]
                near = d + (near_v[k] + (edge_v[pos_s[0, k]] + edge_v[pos_s[1, k]]))
                near_v[k] = near
                r = res_v[:, cols]
                return curve + lane_sums(d * near), norm + lane_sums(r * r)

            zero = jnp.zeros((CLASSES, RANK), f32)
            curve, norm = lax.fori_loop(0, LEAVES, finish_leaf, (zero, zero))
            lo_first = spread(as_row(curve + quad, norm), lo_out, lo_in, lo_s, lo_r, 0, lo_id, lo_peer)
        if level == 7:
            row = total(lo_first, lo_in, 0)
            row = row + as_row(group_quad, jnp.zeros_like(group_quad))
            hi_first = spread(row, hi_out, hi_in, hi_s, hi_r, 0, hi_id, hi_peer)
        message.wait_recv()
        weights = part + dot3(split2(tree_in[level, :CLASSES]), (trans_h[level, other], trans_l[level, other]))
        theirs = tree_in[level, CLASSES:]
        low = jnp.where(half == 1, theirs, points)
        high = jnp.where(half == 1, points, theirs)
        points = pick(jnp.concatenate([low, high], axis=1), hots[level])

    couple = dot3(split2(weights), split2(gaussian(points)))
    descent = descent + dot3(split2(couple), matrix, NT)
    top = as_row(weights * couple, jnp.zeros_like(couple))
    dh, dl = split2(descent)
    both = jnp.concatenate([dh, dl], axis=0)

    row = total(hi_first, hi_in, 0) + top
    sums = as_columns(row)
    norm_old = sums[CLASSES:]
    step_size = norm_old / sums[:CLASSES]
    wide_step = jnp.concatenate([step_size, step_size], axis=1)

    def update(k, norm):
        cols = pl.ds(pl.multiple_of(k * WIDTH, WIDTH), WIDTH)
        bh = basis_h[:, cols]
        far = dot(both, bh)
        far = far[:CLASSES] + far[CLASSES:] + dot(dh, basis_l[:, cols])
        new = res_v[:, cols] - wide_step * (near_v[k] + far)
        nr_ref[:, cols] = new
        return norm + lane_sums(new * new)

    norm = lax.fori_loop(0, LEAVES, update, jnp.zeros((CLASSES, RANK), f32))
    row = as_row(norm, jnp.zeros_like(norm))
    lo_second = spread(row, lo_out, lo_in, lo_s, lo_r, 1, lo_id, lo_peer)
    row = total(lo_second, lo_in, 1)
    hi_second = spread(row, hi_out, hi_in, hi_s, hi_r, 1, hi_id, hi_peer)
    row = total(hi_second, hi_in, 1)
    ab_ref[0] = step_size
    ab_ref[1] = as_columns(row)[:CLASSES] / norm_old

    for message in sent + halo_copies:
        message.wait_send()
    for started in (lo_first, hi_first, lo_second, hi_second):
        for send, _ in started:
            send.wait_send()


def on_device(
    features, solution, residual, direction, neighbours,
    skeleton_basis, base_skeleton, upper_skeleton, transfer,
):
    classes, points = direction.shape
    vmem = pl.BlockSpec(memory_space=pltpu.VMEM)
    whole = pl.BlockSpec(memory_space=pl.ANY)
    dma = pltpu.SemaphoreType.DMA
    new_residual, factors = pl.pallas_call(
        kernel,
        out_shape=(
            jax.ShapeDtypeStruct((classes, points), f32),
            jax.ShapeDtypeStruct((2, classes, RANK), f32),
        ),
        in_specs=[pl.BlockSpec(memory_space=pltpu.SMEM), vmem, vmem, vmem, whole, whole, whole, whole],
        out_specs=(vmem, vmem),
        scratch_shapes=[
            pltpu.VMEM((classes, points), f32),
            pltpu.VMEM((classes, points), f32),
            pltpu.VMEM((RANK, points), f32),
            pltpu.VMEM((LEVELS, 2 * RANK, RANK), f32),
            pltpu.VMEM((RANK, points), bf16),
            pltpu.VMEM((RANK, points), bf16),
            pltpu.VMEM((LEVELS, 2 * RANK, RANK), bf16),
            pltpu.VMEM((LEVELS, 2 * RANK, RANK), bf16),
            pltpu.VMEM((LEVELS, 2 * RANK, RANK), bf16),
            pltpu.VMEM((LEAVES, WIDTH, 16), bf16),
            pltpu.VMEM((LEAVES, 16, WIDTH), bf16),
            pltpu.VMEM((LEAVES, CLASSES + 16, WIDTH), bf16),
            pltpu.VMEM((LEAVES, CLASSES, WIDTH), f32),
            pltpu.VMEM((9, CLASSES, WIDTH), f32),
            pltpu.SMEM((2, LEAVES), jnp.int32),
            pltpu.VMEM((LEVELS, CLASSES + DIMS, RANK), f32),
            pltpu.VMEM((LEVELS, CLASSES + DIMS, RANK), f32),
            pltpu.VMEM((2, BOUND, CLASSES + 16, WIDTH), bf16),
            pltpu.VMEM((2, BOUND, CLASSES + 16, WIDTH), bf16),
            pltpu.VMEM((2, 1, RANK), f32),
            pltpu.VMEM((2, GROUP, 1, RANK), f32),
            pltpu.VMEM((2, 1, RANK), f32),
            pltpu.VMEM((2, GROUP, 1, RANK), f32),
            dma((7,)),
            dma((LEVELS,)),
            dma((LEVELS,)),
            dma((2,)),
            dma((2,)),
            dma((2, GROUP)),
            dma((2, GROUP)),
            dma((2, GROUP)),
            dma((2, GROUP)),
        ],
        compiler_params=pltpu.CompilerParams(
            collective_id=0, has_side_effects=True, vmem_limit_bytes=40 * 1024 * 1024
        ),
        name="cg_step",
    )(neighbours, base_skeleton, upper_skeleton, features, direction, residual, skeleton_basis, transfer)
    step_size = factors[0, :, :1]
    ratio = factors[1, :, :1]
    new_solution = solution + step_size * direction
    new_direction = new_residual + ratio * direction
    return (new_solution, new_residual, new_direction)


def solution(mesh):
    placed = (
        P(None, "leaf"),
        P(None, "leaf"),
        P(None, "leaf"),
        P(None, "leaf"),
        P("leaf", None),
        P(None, "leaf"),
        P("leaf", None),
        P("leaf", None, None),
        P("leaf", None, None, None),
    )
    return jax.shard_map(
        on_device,
        mesh=mesh,
        in_specs=placed,
        out_specs=(P(None, "leaf"), P(None, "leaf"), P(None, "leaf")),
        check_vma=False,
    )
```

time: 504 us -> 74 us (0.15)
  blocking collectives: 155 us -> 0 us
  local copies, waits for them, and re-layouts: 113 us -> 9.34 us
  matrix products: 97.4 us -> 0 us
  Pallas kernels: 0 us -> 62.1 us
  starting transfers between devices: 53.6 us -> 0 us
  loops' own time: 34.3 us -> 0 us
  other arithmetic: 24.2 us -> 1.57 us
  waiting for transfers between devices: 21.2 us -> 0 us
    psum x2 -> x0, blocking collectives: 155 us -> none  [the longest x1 82.1 us: on_device(): norm_old = lax.psum(jnp.sum(residual * residual, axis=1), 'leaf')]
    dot_general x68 -> x0, matrix products: 97.4 us -> none  [the longest x16 36.4 us: leaf_near(): jnp.einsum('rsj,sji->ri', weighted, tile_block, preferred_element_type=jn...]
    gather x57 -> x0, local copies, waits for them, and re-layouts: 73.8 us -> none  [the longest x16 31.5 us: tile_terms(): jnp.take(pool_values, spot_ids, axis=1)]
    pallas_call x0 -> x1, Pallas kernels: none -> 62.1 us  [on_device(): pl.pallas_call(kernel, out_shape=(jax.ShapeDtypeStruct((classes, points),...]
    ppermute x20 -> x0, starting transfers between devices: 53.6 us -> none  [the longest x16 41.2 us: from_partner(): return lax.ppermute(value, axis, pairs)]
    another operation x1 -> x0, loops' own time: 34.3 us -> none  [on_device(): near_rows = lax.map(leaf_near, jnp.arange(leaves))]
    ppermute x20 -> x0, waiting for transfers between devices: 21.2 us -> none  [the longest x16 21.2 us: from_partner(): return lax.ppermute(value, axis, pairs)]
    dynamic_slice x16 -> x0, local copies, waits for them, and re-layouts: 21 us -> none  [on_device(): near_rows = lax.map(leaf_near, jnp.arange(leaves))]
  transfers between devices with their start and end apart: 20 -> 0, of which waited for: 13 -> 0; matrix products, arithmetic and copies ran while one was open for 11% -> 0% of each run, Pallas kernels for 0% -> 0%
where the time goes in v1:
time: 74 us; the launch traced here: 73.7 us
  Pallas kernels  62.1 us (84%)
  local copies, waits for them, and re-layouts  9.34 us (13%)
  other arithmetic  1.57 us (2%)
    pallas_call x1, Pallas kernels, on_device(): pl.pallas_call(kernel, out_shape=(jax.ShapeDtypeStruct((classes, points),...  62.1 us
    unnamed x18, local copies, waits for them, and re-layouts  9.24 us
    add x1, other arithmetic, on_device(): new_direction = new_residual + ratio * direction  1.57 us

profile of v1, /device:TPU:1, one launch (start us, length us, event | category | flops | bytes accessed | tf_op | source)
XLA Modules:
  0.0 73.7 jit_solution(6295965174550850483)
XLA Ops:
  0.6 0.8 %copy.13.nbr = s32[16,8]{1,0:T(8,128)S(1)} copy(s32[16,8]{0,1:T(8,128)} %param.13) | data formatting | bytes 1024 | tf_op args[4]
  1.4 0.0 copy-start
  1.4 1.2 %copy-done = f32[64,4096]{1,0:T(8,128)S(1)} copy-done((f32[64,4096]{1,0:T(8,128)S(1)}, f32[64,4096]{1,0:T(8,128)}, u32[]{:S(2)}) %copy-start) | copy-done | bytes 1048600
  2.6 0.0 copy-start.1
  2.6 1.6 %copy-done.1 = f32[128,4096]{1,0:T(8,128)S(1)} copy-done((f32[128,4096]{1,0:T(8,128)S(1)}, f32[128,4096]{1,0:T(8,128)}, u32[]{:S(2)}) %copy-start.1) | copy-done | bytes 2097176
  4.2 0.0 copy-start.2
  4.2 1.2 %copy-done.2 = f32[64,4096]{1,0:T(8,128)S(1)} copy-done((f32[64,4096]{1,0:T(8,128)S(1)}, f32[64,4096]{1,0:T(8,128)}, u32[]{:S(2)}) %copy-start.2) | copy-done | bytes 1048600
  5.4 0.0 copy-start.3
  5.4 1.2 %copy-done.3 = f32[1,8,256,128]{3,2,1,0:T(8,128)S(1)} copy-done((f32[1,8,256,128]{3,2,1,0:T(8,128)S(1)}, f32[1,8,256,128]{3,2,1,0:T(8,128)}, u32[]{:S(2)}) %copy-start.3) | copy-done | bytes 1048600
  6.7 0.0 copy-start.4
  6.7 0.9 %copy-done.4 = f32[8,4096]{1,0:T(8,128)S(1)} copy-done((f32[8,4096]{1,0:T(8,128)S(1)}, f32[8,4096]{1,0:T(8,128)}, u32[]{:S(2)}) %copy-start.4) | copy-done | bytes 131096
  7.6 0.0 copy-start.5
  7.6 0.7 copy-done.5
  8.2 0.0 copy-start.6
  8.2 0.7 copy-done.6
  8.9 0.0 copy-start.7
  8.9 62.1 %cg_step.1 = (f32[64,4096]{1,0:T(8,128)S(1)}, f32[2,64,128]{2,1,0:T(8,128)S(1)}) custom-call(s32[16,8]{1,0:T(8,128)S(1)} %copy.13.nbr, s32[1,128]{1,0:T(1,128)S(1)} %copy-done.6, s32[1,8,128]{2,1,0:T(8,128)S(1)} %copy-done.5, f32[8,4096]{1,0:T(8,128)S(1)} %copy-done.4, f32[64,4096]{1,0:T(8,128)S(1)} %copy-done, f32[64,4096]{1,0:T(8,128)S(1)} %copy-done.2, ...), custom_call_target="tpu_custom_call" | custom-call | tf_op jit(solution)/shard_map/cg_step/pallas_call | solution.py:392
  71.1 0.1 slice_reduce_fusion
  71.2 0.0 copy-done.7
  71.2 1.6 %multiply_add_fusion = (f32[64,4096]{1,0:T(8,128)}, f32[64,4096]{1,0:T(8,128)}) fusion(f32[64,4096]{1,0:T(8,128)S(1)} %get-tuple-element.15, f32[64,4096]{1,0:T(8,128)S(1)} %copy-done, f32[64]{0:T(128)S(1)} %get-tuple-element.7, f32[64,4096]{1,0:T(8,128)S(1)} %copy-done.7, f32[64]{0:T(128)S(1)} %get-tuple-element.8), kind=kLoop, calls=%fused_computation | loop fusion | flops 1048576 | bytes 5243392 | tf_op jit(solution)/shard_map/add | solution.py:442
  72.8 1.0 %copy.15 = f32[64,4096]{1,0:T(8,128)} copy(f32[64,4096]{1,0:T(8,128)S(1)} %get-tuple-element.15) | data formatting | bytes 2097152
Async XLA Ops:
  1.4 1.2 %copy-start = (f32[64,4096]{1,0:T(8,128)S(1)}, f32[64,4096]{1,0:T(8,128)}, u32[]{:S(2)}) copy-start(f32[64,4096]{1,0:T(8,128)} %dir_any.1) | copy-start | bytes 3145732
  2.6 1.6 %copy-start.1 = (f32[128,4096]{1,0:T(8,128)S(1)}, f32[128,4096]{1,0:T(8,128)}, u32[]{:S(2)}) copy-start(f32[128,4096]{1,0:T(8,128)} %basis_any.1) | copy-start | bytes 6291460
  4.2 1.2 %copy-start.2 = (f32[64,4096]{1,0:T(8,128)S(1)}, f32[64,4096]{1,0:T(8,128)}, u32[]{:S(2)}) copy-start(f32[64,4096]{1,0:T(8,128)} %res_any.1) | copy-start | bytes 3145732
  5.4 1.2 %copy-start.3 = (f32[1,8,256,128]{3,2,1,0:T(8,128)S(1)}, f32[1,8,256,128]{3,2,1,0:T(8,128)}, u32[]{:S(2)}) copy-start(f32[1,8,256,128]{3,2,1,0:T(8,128)} %trans_any.1) | copy-start | bytes 3145732
  6.7 0.9 %copy-start.4 = (f32[8,4096]{1,0:T(8,128)S(1)}, f32[8,4096]{1,0:T(8,128)}, u32[]{:S(2)}) copy-start(f32[8,4096]{1,0:T(8,128)} %feat_ref.1) | copy-start | bytes 393220
  7.6 0.7 copy-start.5
  8.2 0.7 copy-start.6
  8.9 62.3 %copy-start.7 = (f32[64,4096]{1,0:T(8,128)S(1)}, f32[64,4096]{1,0:T(8,128)}, u32[]{:S(2)}) copy-start(f32[64,4096]{1,0:T(8,128)} %param.10) | copy-start | bytes 3145732

commit v2 on v1

--- a/solution.py
+++ b/solution.py
@@ -23,8 +23,12 @@
 CLASSES = 64
 DIMS = 8
 CHUNK = 512
+FINISH = 1024
 MASKS = (1, 2, 4, 14, 16, 48, 64, 192)
-SHARE = (0, 2, 4, 4, 3, 3, 0, 0)
+TEAM = 4
+TILES = INNER + 1
+STEPS = LEAVES // TEAM * TILES // 2
+SHARE = (0, 2, 3, 4, 3, 2, 0, 0)
 
 
 def flip(me, mask):
@@ -95,10 +99,10 @@
 
 
 def kernel(
-    nbr, base_ref, upper_ref, feat_ref, dir_any, res_any, basis_any, trans_any,
+    nbr_any, base_ref, upper_ref, feat_ref, dir_any, res_any, basis_any, trans_any,
     nr_ref, ab_ref,
     dir_v, res_v, basis_v, trans_v, basis_h, basis_l, trans_h, trans_l, hots,
-    source_v, target_v, value_v, near_v, edge_v, pos_s,
+    source_v, target_v, value_v, near_v, edge_v, tile_v, nbr, pos_s,
     tree_out, tree_in, halo_out, halo_in, lo_out, lo_in, hi_out, hi_in,
     local_sem, tree_s, tree_r, halo_s, halo_r, lo_s, lo_r, hi_s, hi_r,
 ):
@@ -108,6 +112,8 @@
     halves = [me // 2**level % 2 for level in range(LEVELS)]
 
     copies = {}
+    copies["nbr"] = pltpu.make_async_copy(nbr_any, nbr, local_sem.at[7])
+    copies["nbr"].start()
     quarter = basis_v.shape[1] // 4
     copies["dir"] = pltpu.make_async_copy(dir_any, dir_v, local_sem.at[0])
     copies["dir"].start()
@@ -129,6 +135,7 @@
     for peer in peers:
         pl.semaphore_signal(barrier, inc=1, device_id=(peer,), device_id_type=MESH)
 
+    copies["nbr"].wait()
     edges = []
     for slot in (6, 7):
         count = jnp.int32(0)
@@ -190,24 +197,40 @@
     def tile(source, k):
         return jnp.exp(dot(source, target_v[k])).astype(bf16)
 
-    def near_leaf(k, carry):
-        own = dot(value_v[k, :CLASSES, :], tile(source_v[k], k))
-        sides = jnp.zeros((CLASSES, WIDTH), f32)
-        for s in range(INNER):
-            partner = nbr[k, s]
-            filled = partner >= 0
-            j = jnp.clip(partner - me * LEAVES, 0, LEAVES - 1)
-            scale = jnp.where(filled, 0.125, 0.0).astype(f32)
-            sides = sides + scale * dot(value_v[j, :CLASSES, :], tile(source_v[j], k))
-        near_v[k] = own + sides
+    def near_place(batch, member):
+        slot = batch % TILES
+        k = batch // TILES * TEAM + member
+        partner = nbr[k, jnp.maximum(slot - 1, 0)]
+        j = jnp.where(slot == 0, k, jnp.clip(partner - me * LEAVES, 0, LEAVES - 1))
+        scale = jnp.where(slot == 0, 1.0, jnp.where(partner >= 0, 0.125, 0.0)).astype(f32)
+        return k, j, scale
+
+    def near_add(batch, buffer):
+        for member in range(TEAM):
+            k, j, scale = near_place(batch, member)
+            near_v[k] = near_v[k] + scale * dot(value_v[j, :CLASSES, :], tile_v[buffer, member])
+
+    def near_batch(batch, buffer):
+        near_add(jnp.maximum(batch - 1, 0), 1 - buffer)
+        for member in range(TEAM):
+            k, j, _ = near_place(batch, member)
+            tile_v[buffer, member] = tile(source_v[j], k)
+
+    def near_step(step, carry):
+        near_batch(2 * step, 0)
+        near_batch(2 * step + 1, 1)
         return carry
 
-    def near_edge(side, at):
-        mine, ranks = edges[side]
-        for q in range(BOUND):
-            block = halo_in[side, ranks[q]]
-            source = block[CLASSES:].astype(f32).T.astype(bf16)
-            edge_v[at + q] = 0.125 * dot(block[:CLASSES], tile(source, mine[q]))
+    def near_edges():
+        for side, at in ((1, 0), (0, 5)):
+            mine, ranks = edges[side]
+            for q in range(BOUND):
+                source = halo_in[side, ranks[q], CLASSES:].astype(f32).T.astype(bf16)
+                tile_v[side, q] = tile(source, mine[q])
+        for side, at in ((1, 0), (0, 5)):
+            ranks = edges[side][1]
+            for q in range(BOUND):
+                edge_v[at + q] = 0.125 * dot(halo_in[side, ranks[q], :CLASSES], tile_v[side, q])
 
     def lane_sums(x):
         out = x[:, :RANK]
@@ -273,6 +296,8 @@
         message.start()
         sent.append(message)
         if level == 0:
+            near_v[...] = jnp.zeros_like(near_v)
+            tile_v[1] = jnp.zeros((TEAM, WIDTH, WIDTH), bf16)
             copies["trans"].wait()
             for i in range(LEVELS):
                 th, tl = split2(trans_v[i])
@@ -310,14 +335,15 @@
         else:
             matrix = split2(dot3(matrix, step))
         if SHARE[level]:
-            lax.fori_loop(done, done + SHARE[level], near_leaf, 0)
+            lax.fori_loop(done, done + SHARE[level], near_step, 0)
             done += SHARE[level]
-        if level == 3:
+            if done == STEPS:
+                near_add(2 * STEPS - 1, 1)
+        if level == 5:
             halo_copies[0].wait_recv()
             halo_copies[1].wait_recv()
-            edge_v[4] = jnp.zeros((CLASSES, WIDTH), f32)
-            near_edge(1, 0)
-            near_edge(0, 5)
+            edge_v[BOUND] = jnp.zeros((CLASSES, WIDTH), f32)
+            near_edges()
         if level == 6:
             copies["res"].wait()
 
@@ -350,6 +376,14 @@
     dh, dl = split2(descent)
     both = jnp.concatenate([dh, dl], axis=0)
 
+    def image(k, carry):
+        cols = pl.ds(pl.multiple_of(k * WIDTH, WIDTH), WIDTH)
+        far = dot(both, basis_h[:, cols])
+        far = far[:CLASSES] + far[CLASSES:] + dot(dh, basis_l[:, cols])
+        near_v[k] = near_v[k] + far
+        return carry
+
+    lax.fori_loop(0, LEAVES, image, 0, unroll=2)
     row = total(hi_first, hi_in, 0) + top
     sums = as_columns(row)
     norm_old = sums[CLASSES:]
@@ -358,10 +392,7 @@
 
     def update(k, norm):
         cols = pl.ds(pl.multiple_of(k * WIDTH, WIDTH), WIDTH)
-        bh = basis_h[:, cols]
-        far = dot(both, bh)
-        far = far[:CLASSES] + far[CLASSES:] + dot(dh, basis_l[:, cols])
-        new = res_v[:, cols] - wide_step * (near_v[k] + far)
+        new = res_v[:, cols] - wide_step * near_v[k]
         nr_ref[:, cols] = new
         return norm + lane_sums(new * new)
 
@@ -379,6 +410,15 @@
     for started in (lo_first, hi_first, lo_second, hi_second):
         for send, _ in started:
             send.wait_send()
+
+
+def finish(factors, sol_ref, nr_ref, dir_ref, new_sol_ref, new_res_ref, new_dir_ref):
+    wide = lambda x: jnp.concatenate([x] * (FINISH // RANK), axis=1)
+    d = dir_ref[...]
+    nr = nr_ref[...]
+    new_sol_ref[...] = sol_ref[...] + wide(factors[0]) * d
+    new_res_ref[...] = nr
+    new_dir_ref[...] = nr + wide(factors[1]) * d
 
 
 def on_device(
@@ -395,7 +435,7 @@
             jax.ShapeDtypeStruct((classes, points), f32),
             jax.ShapeDtypeStruct((2, classes, RANK), f32),
         ),
-        in_specs=[pl.BlockSpec(memory_space=pltpu.SMEM), vmem, vmem, vmem, whole, whole, whole, whole],
+        in_specs=[whole, vmem, vmem, vmem, whole, whole, whole, whole],
         out_specs=(vmem, vmem),
         scratch_shapes=[
             pltpu.VMEM((classes, points), f32),
@@ -412,6 +452,8 @@
             pltpu.VMEM((LEAVES, CLASSES + 16, WIDTH), bf16),
             pltpu.VMEM((LEAVES, CLASSES, WIDTH), f32),
             pltpu.VMEM((9, CLASSES, WIDTH), f32),
+            pltpu.VMEM((2, TEAM, WIDTH, WIDTH), bf16),
+            pltpu.SMEM((LEAVES, 8), jnp.int32),
             pltpu.SMEM((2, LEAVES), jnp.int32),
             pltpu.VMEM((LEVELS, CLASSES + DIMS, RANK), f32),
             pltpu.VMEM((LEVELS, CLASSES + DIMS, RANK), f32),
@@ -421,7 +463,7 @@
             pltpu.VMEM((2, GROUP, 1, RANK), f32),
             pltpu.VMEM((2, 1, RANK), f32),
             pltpu.VMEM((2, GROUP, 1, RANK), f32),
-            dma((7,)),
+            dma((8,)),
             dma((LEVELS,)),
             dma((LEVELS,)),
             dma((2,)),
@@ -432,15 +474,19 @@
             dma((2, GROUP)),
         ],
         compiler_params=pltpu.CompilerParams(
-            collective_id=0, has_side_effects=True, vmem_limit_bytes=40 * 1024 * 1024
+            collective_id=0, has_side_effects=True, vmem_limit_bytes=60 * 1024 * 1024
         ),
         name="cg_step",
     )(neighbours, base_skeleton, upper_skeleton, features, direction, residual, skeleton_basis, transfer)
-    step_size = factors[0, :, :1]
-    ratio = factors[1, :, :1]
-    new_solution = solution + step_size * direction
-    new_direction = new_residual + ratio * direction
-    return (new_solution, new_residual, new_direction)
+    block = pl.BlockSpec((classes, FINISH), lambda i: (0, i))
+    return pl.pallas_call(
+        finish,
+        grid=(points // FINISH,),
+        out_shape=[jax.ShapeDtypeStruct((classes, points), f32)] * 3,
+        in_specs=[pl.BlockSpec((2, classes, RANK), lambda i: (0, 0, 0)), block, block, block],
+        out_specs=[block] * 3,
+        name="cg_finish",
+    )(factors, solution, new_residual, direction)
 
 
 def solution(mesh):

time: 74 us -> 59.1 us (0.80)
  local copies, waits for them, and re-layouts: 9.34 us -> 1.36 us
  Pallas kernels: 62.1 us -> 56.9 us
  other arithmetic: 1.57 us -> 0 us
    pallas_call x1, Pallas kernels: 62.1 us -> 52.7 us  [on_device(): pl.pallas_call(kernel, out_shape=(jax.ShapeDtypeStruct((classes, points),...]
    unnamed x18 -> x1, local copies, waits for them, and re-layouts: 9.24 us -> 1.36 us
    pallas_call x0 -> x1, Pallas kernels: none -> 4.21 us  [on_device(): pl.pallas_call(finish, grid=(points // FINISH,), out_shape=[jax.ShapeDtyp...]
    add x1 -> x0, other arithmetic: 1.57 us -> none  [on_device(): new_direction = new_residual + ratio * direction]
where the time goes in v2:
time: 59.1 us; the launch traced here: 58.9 us
  Pallas kernels  56.9 us (96%)
  local copies, waits for them, and re-layouts  1.36 us (2%)
  between operations  0.64 us (1%)
    pallas_call x1, Pallas kernels, on_device(): pl.pallas_call(kernel, out_shape=(jax.ShapeDtypeStruct((classes, points),...  52.7 us
    pallas_call x1, Pallas kernels, on_device(): pl.pallas_call(finish, grid=(points // FINISH,), out_shape=[jax.ShapeDtyp...  4.21 us
    unnamed x1, local copies, waits for them, and re-layouts  1.36 us

profile of v2, /device:TPU:1, one launch (start us, length us, event | category | flops | bytes accessed | tf_op | source)
XLA Modules:
  0.0 58.9 jit_solution(240670041874517842)
XLA Ops:
  0.6 1.4 %copy.12.nbr_any = s32[16,8]{1,0:T(8,128)} copy(s32[16,8]{0,1:T(8,128)} %param.13) | data formatting | bytes 1024 | tf_op args[4]
  2.0 52.7 %cg_step.1 = (f32[64,4096]{1,0:T(8,128)}, f32[2,64,128]{2,1,0:T(8,128)}) custom-call(s32[16,8]{1,0:T(8,128)} %copy.12.nbr_any, s32[1,128]{1,0:T(1,128)} %base_ref.1, s32[1,8,128]{2,1,0:T(8,128)} %upper_ref.1, f32[8,4096]{1,0:T(8,128)} %feat_ref.1, f32[64,4096]{1,0:T(8,128)} %dir_ref.1, f32[64,4096]{1,0:T(8,128)} %res_any.1, f32[128,4096]{1,0:T(8,128)} %basis_any.1, ...), custom_call_target="tpu_custom_call" | custom-call | tf_op jit(solution)/shard_map/cg_step/pallas_call | solution.py:432
  54.7 4.2 %cg_finish.1 = (f32[64,4096]{1,0:T(8,128)}, f32[64,4096]{1,0:T(8,128)}, f32[64,4096]{1,0:T(8,128)}) custom-call(f32[2,64,128]{2,1,0:T(8,128)} %get-tuple-element.5.factors, f32[64,4096]{1,0:T(8,128)} %sol_ref.1, f32[64,4096]{1,0:T(8,128)} %get-tuple-element.6.nr_ref, f32[64,4096]{1,0:T(8,128)} %dir_ref.1), custom_call_target="tpu_custom_call" | custom-call | tf_op jit(solution)/shard_map/cg_finish/pallas_call | solution.py:482

commit v3 on v2

--- a/solution.py
+++ b/solution.py
@@ -23,12 +23,14 @@
 CLASSES = 64
 DIMS = 8
 CHUNK = 512
-FINISH = 1024
-MASKS = (1, 2, 4, 14, 16, 48, 64, 192)
+FINISH = 2048
+STAGES = ((1,), (2, 4, 6), (14,), (16, 32, 48), (64, 128, 192))
+FAR_FIRST = (8, 7, 9, 6, 10, 5, 11, 4, 12, 3, 13, 2, 14, 1, 15)
+MESSAGES = sum(len(stage) for stage in STAGES)
 TEAM = 4
 TILES = INNER + 1
 STEPS = LEAVES // TEAM * TILES // 2
-SHARE = (0, 2, 3, 4, 3, 2, 0, 0)
+SHARE = (0, 5, 4, 5, 0)
 
 
 def flip(me, mask):
@@ -103,7 +105,7 @@
     nr_ref, ab_ref,
     dir_v, res_v, basis_v, trans_v, basis_h, basis_l, trans_h, trans_l, hots,
     source_v, target_v, value_v, near_v, edge_v, tile_v, nbr, pos_s,
-    tree_out, tree_in, halo_out, halo_in, lo_out, lo_in, hi_out, hi_in,
+    node_v, descent_v, tree_out, tree_in, halo_out, halo_in, lo_out, lo_in, hi_out, hi_in,
     local_sem, tree_s, tree_r, halo_s, halo_r, lo_s, lo_r, hi_s, hi_r,
 ):
     me = lax.axis_index("leaf")
@@ -142,7 +144,7 @@
         mine = [jnp.int32(0)] * BOUND
         theirs = [jnp.int32(0)] * BOUND
         for k in range(LEAVES):
-            partner = nbr[k, slot]
+            partner = nbr[slot, k]
             filled = partner >= 0
             place = jnp.minimum(count, BOUND - 1) + (BOUND + 1 if slot == 6 else 0)
             pos_s[slot - 6, k] = jnp.where(filled, place, BOUND)
@@ -200,7 +202,7 @@
     def near_place(batch, member):
         slot = batch % TILES
         k = batch // TILES * TEAM + member
-        partner = nbr[k, jnp.maximum(slot - 1, 0)]
+        partner = nbr[jnp.maximum(slot - 1, 0), k]
         j = jnp.where(slot == 0, k, jnp.clip(partner - me * LEAVES, 0, LEAVES - 1))
         scale = jnp.where(slot == 0, 1.0, jnp.where(partner >= 0, 0.125, 0.0)).astype(f32)
         return k, j, scale
@@ -248,7 +250,7 @@
         out[use] = row
         into[use, own_id] = row
         started = []
-        for m in range(1, GROUP):
+        for m in FAR_FIRST:
             peer, slot = where(m)
             send = pltpu.make_async_remote_copy(
                 src_ref=out.at[use], dst_ref=into.at[use, own_id],
@@ -277,102 +279,141 @@
             arrival.wait_recv()
         return jnp.sum(into[use], axis=0)
 
+    def halo_start():
+        started = []
+        for side, target in ((0, left), (1, right)):
+            leaves = edges[side][0]
+            for q in range(BOUND):
+                halo_out[side, q] = value_v[leaves[q]]
+            halo = pltpu.make_async_remote_copy(
+                src_ref=halo_out.at[side], dst_ref=halo_in.at[1 - side],
+                send_sem=halo_s.at[side], recv_sem=halo_r.at[1 - side],
+                device_id=(target,), device_id_type=MESH,
+            )
+            halo.start()
+            started.append(halo)
+        return started
+
+    def split_level(level):
+        th, tl = split2(trans_v[level])
+        trans_h[level] = th
+        trans_l[level] = tl
+        hots[level] = one_hot(upper_ref[0, level : level + 1, :], 0, 2 * RANK)
+
+    def raised(level, half, node):
+        rows = pl.ds(pl.multiple_of(half * RANK, RANK), RANK)
+        step = (trans_h[level, rows], trans_l[level, rows])
+        return (
+            dot3(split2(node[0]), step),
+            pick(node[1], hots[level, rows]),
+        )
+
+    def plus(a, b):
+        return (a[0] + b[0], a[1] + b[1])
+
+    def keep(level, node):
+        node_v[level, :CLASSES] = node[0]
+        node_v[level, CLASSES:] = node[1]
+
+    def coupled(level, matrix):
+        weights = node_v[level, :CLASSES]
+        couple = dot3(split2(weights), split2(gaussian(node_v[level, CLASSES:])))
+        if level == 0:
+            descent_v[0] = couple
+            return None, weights * couple
+        half = halves[level - 1]
+        rows = pl.ds(pl.multiple_of(half * RANK, RANK), RANK)
+        if level == 1:
+            matrix = trans_v[0, rows]
+        else:
+            matrix = dot3(split2(matrix), (trans_h[level - 1, rows], trans_l[level - 1, rows]))
+        descent_v[level] = dot3(split2(couple), split2(matrix.T))
+        return matrix, weights * couple
+
+    def finish_near():
+        def finish_leaf(k, carry):
+            curve, norm = carry
+            cols = pl.ds(pl.multiple_of(k * WIDTH, WIDTH), WIDTH)
+            d = dir_v[:, cols]
+            near = d + (near_v[k] + (edge_v[pos_s[0, k]] + edge_v[pos_s[1, k]]))
+            near_v[k] = near
+            r = res_v[:, cols]
+            return curve + lane_sums(d * near), norm + lane_sums(r * r)
+
+        zero = jnp.zeros((CLASSES, RANK), f32)
+        return lax.fori_loop(0, LEAVES, finish_leaf, (zero, zero))
+
     sent = []
-    lo_first = hi_first = None
-    halo_copies = []
+    level = 0
+    slot = 0
     done = 0
-    matrix = None
-    descent = None
-    quad = jnp.zeros((CLASSES, RANK), f32)
-    group_quad = jnp.zeros((CLASSES, RANK), f32)
-    for level in range(LEVELS):
-        tree_out[level, :CLASSES] = weights
-        tree_out[level, CLASSES:] = points
-        message = pltpu.make_async_remote_copy(
-            src_ref=tree_out.at[level], dst_ref=tree_in.at[level],
-            send_sem=tree_s.at[level], recv_sem=tree_r.at[level],
-            device_id=(flip(me, MASKS[level]),), device_id_type=MESH,
-        )
-        message.start()
-        sent.append(message)
-        if level == 0:
+    node = (weights, points)
+    keep(0, node)
+    copies["trans"].wait()
+    split_level(0)
+    for stage, masks in enumerate(STAGES):
+        gift = raised(level, halves[level], node)
+        tree_out[stage, :CLASSES] = gift[0]
+        tree_out[stage, CLASSES:] = gift[1]
+        messages = []
+        for mask in masks:
+            message = pltpu.make_async_remote_copy(
+                src_ref=tree_out.at[stage], dst_ref=tree_in.at[slot],
+                send_sem=tree_s.at[slot], recv_sem=tree_r.at[slot],
+                device_id=(flip(me, mask),), device_id_type=MESH,
+            )
+            message.start()
+            messages.append((message, slot))
+            slot += 1
+        sent += [message for message, _ in messages]
+        if stage == 0:
+            for i in range(1, LEVELS):
+                split_level(i)
             near_v[...] = jnp.zeros_like(near_v)
             tile_v[1] = jnp.zeros((TEAM, WIDTH, WIDTH), bf16)
-            copies["trans"].wait()
-            for i in range(LEVELS):
-                th, tl = split2(trans_v[i])
-                trans_h[i] = th
-                trans_l[i] = tl
-                hots[i] = one_hot(upper_ref[0, i : i + 1, :], 0, 2 * RANK)
-        half = halves[level]
-        mine = pl.ds(pl.multiple_of(half * RANK, RANK), RANK)
-        other = pl.ds(pl.multiple_of((1 - half) * RANK, RANK), RANK)
-        step = (trans_h[level, mine], trans_l[level, mine])
-        part = dot3(split2(weights), step)
-        if level == 0:
-            for side, target in ((0, left), (1, right)):
-                leaves = edges[side][0]
-                for q in range(BOUND):
-                    halo_out[side, q] = value_v[leaves[q]]
-                halo = pltpu.make_async_remote_copy(
-                    src_ref=halo_out.at[side], dst_ref=halo_in.at[1 - side],
-                    send_sem=halo_s.at[side], recv_sem=halo_r.at[1 - side],
-                    device_id=(target,), device_id_type=MESH,
-                )
-                halo.start()
-                halo_copies.append(halo)
-        couple = dot3(split2(weights), split2(gaussian(points)))
-        if level == 0:
-            descent = couple
-        else:
-            descent = descent + dot3(split2(couple), matrix, NT)
-        if level < 4:
-            quad = quad + 0.5**level * (weights * couple)
-        else:
-            group_quad = group_quad + 0.5 ** (level - 4) * (weights * couple)
-        if level == 0:
-            matrix = step
-        else:
-            matrix = split2(dot3(matrix, step))
-        if SHARE[level]:
-            lax.fori_loop(done, done + SHARE[level], near_step, 0)
-            done += SHARE[level]
+        if stage == 2:
+            halo_copies = halo_start()
+        if SHARE[stage]:
+            lax.fori_loop(done, done + SHARE[stage], near_step, 0)
+            done += SHARE[stage]
             if done == STEPS:
                 near_add(2 * STEPS - 1, 1)
-        if level == 5:
+        if stage == 3:
             halo_copies[0].wait_recv()
             halo_copies[1].wait_recv()
             edge_v[BOUND] = jnp.zeros((CLASSES, WIDTH), f32)
             near_edges()
-        if level == 6:
             copies["res"].wait()
-
-            def finish_leaf(k, carry):
-                curve, norm = carry
-                cols = pl.ds(pl.multiple_of(k * WIDTH, WIDTH), WIDTH)
-                d = dir_v[:, cols]
-                near = d + (near_v[k] + (edge_v[pos_s[0, k]] + edge_v[pos_s[1, k]]))
-                near_v[k] = near
-                r = res_v[:, cols]
-                return curve + lane_sums(d * near), norm + lane_sums(r * r)
-
-            zero = jnp.zeros((CLASSES, RANK), f32)
-            curve, norm = lax.fori_loop(0, LEAVES, finish_leaf, (zero, zero))
+            curve, norm = finish_near()
+            matrix, quad = coupled(0, None)
+            for i in range(1, 5):
+                matrix, more = coupled(i, matrix)
+                quad = quad + 0.5**i * more
             lo_first = spread(as_row(curve + quad, norm), lo_out, lo_in, lo_s, lo_r, 0, lo_id, lo_peer)
-        if level == 7:
-            row = total(lo_first, lo_in, 0)
-            row = row + as_row(group_quad, jnp.zeros_like(group_quad))
-            hi_first = spread(row, hi_out, hi_in, hi_s, hi_r, 0, hi_id, hi_peer)
-        message.wait_recv()
-        weights = part + dot3(split2(tree_in[level, :CLASSES]), (trans_h[level, other], trans_l[level, other]))
-        theirs = tree_in[level, CLASSES:]
-        low = jnp.where(half == 1, theirs, points)
-        high = jnp.where(half == 1, points, theirs)
-        points = pick(jnp.concatenate([low, high], axis=1), hots[level])
-
-    couple = dot3(split2(weights), split2(gaussian(points)))
-    descent = descent + dot3(split2(couple), matrix, NT)
-    top = as_row(weights * couple, jnp.zeros_like(couple))
+        if stage == 4:
+            matrix, quad = coupled(5, matrix)
+            matrix, more = coupled(6, matrix)
+            quad = 0.5 * quad + 0.25 * more
+        given = []
+        for message, at in messages:
+            message.wait_recv()
+            given.append((tree_in[at, :CLASSES], tree_in[at, CLASSES:]))
+        node = plus(gift, given[0])
+        level += 1
+        keep(level, node)
+        if len(masks) == 3:
+            other = plus(given[1], given[2])
+            half = halves[level]
+            node = plus(raised(level, half, node), raised(level, 1 - half, other))
+            level += 1
+            keep(level, node)
+
+    matrix, more = coupled(7, matrix)
+    row = total(lo_first, lo_in, 0) + as_row(quad + 0.125 * more, jnp.zeros_like(quad))
+    hi_first = spread(row, hi_out, hi_in, hi_s, hi_r, 0, hi_id, hi_peer)
+    _, top = coupled(8, matrix)
+    top = as_row(top, jnp.zeros_like(top))
+    descent = lax.fori_loop(1, LEVELS + 1, lambda i, total: total + descent_v[i], descent_v[0])
     dh, dl = split2(descent)
     both = jnp.concatenate([dh, dl], axis=0)
 
@@ -399,17 +440,20 @@
     norm = lax.fori_loop(0, LEAVES, update, jnp.zeros((CLASSES, RANK), f32))
     row = as_row(norm, jnp.zeros_like(norm))
     lo_second = spread(row, lo_out, lo_in, lo_s, lo_r, 1, lo_id, lo_peer)
+    for message in sent + halo_copies:
+        message.wait_send()
+    for send, _ in lo_first + hi_first:
+        send.wait_send()
     row = total(lo_second, lo_in, 1)
     hi_second = spread(row, hi_out, hi_in, hi_s, hi_r, 1, hi_id, hi_peer)
+    for send, _ in lo_second:
+        send.wait_send()
     row = total(hi_second, hi_in, 1)
     ab_ref[0] = step_size
     ab_ref[1] = as_columns(row)[:CLASSES] / norm_old
 
-    for message in sent + halo_copies:
-        message.wait_send()
-    for started in (lo_first, hi_first, lo_second, hi_second):
-        for send, _ in started:
-            send.wait_send()
+    for send, _ in hi_second:
+        send.wait_send()
 
 
 def finish(factors, sol_ref, nr_ref, dir_ref, new_sol_ref, new_res_ref, new_dir_ref):
@@ -453,10 +497,12 @@
             pltpu.VMEM((LEAVES, CLASSES, WIDTH), f32),
             pltpu.VMEM((9, CLASSES, WIDTH), f32),
             pltpu.VMEM((2, TEAM, WIDTH, WIDTH), bf16),
-            pltpu.SMEM((LEAVES, 8), jnp.int32),
+            pltpu.SMEM((8, LEAVES), jnp.int32),
             pltpu.SMEM((2, LEAVES), jnp.int32),
-            pltpu.VMEM((LEVELS, CLASSES + DIMS, RANK), f32),
-            pltpu.VMEM((LEVELS, CLASSES + DIMS, RANK), f32),
+            pltpu.VMEM((LEVELS + 1, CLASSES + DIMS, RANK), f32),
+            pltpu.VMEM((LEVELS + 1, CLASSES, RANK), f32),
+            pltpu.VMEM((len(STAGES), CLASSES + DIMS, RANK), f32),
+            pltpu.VMEM((MESSAGES, CLASSES + DIMS, RANK), f32),
             pltpu.VMEM((2, BOUND, CLASSES + 16, WIDTH), bf16),
             pltpu.VMEM((2, BOUND, CLASSES + 16, WIDTH), bf16),
             pltpu.VMEM((2, 1, RANK), f32),
@@ -464,8 +510,8 @@
             pltpu.VMEM((2, 1, RANK), f32),
             pltpu.VMEM((2, GROUP, 1, RANK), f32),
             dma((8,)),
-            dma((LEVELS,)),
-            dma((LEVELS,)),
+            dma((MESSAGES,)),
+            dma((MESSAGES,)),
             dma((2,)),
             dma((2,)),
             dma((2, GROUP)),
@@ -477,7 +523,7 @@
             collective_id=0, has_side_effects=True, vmem_limit_bytes=60 * 1024 * 1024
         ),
         name="cg_step",
-    )(neighbours, base_skeleton, upper_skeleton, features, direction, residual, skeleton_basis, transfer)
+    )(neighbours.T, base_skeleton, upper_skeleton, features, direction, residual, skeleton_basis, transfer)
     block = pl.BlockSpec((classes, FINISH), lambda i: (0, i))
     return pl.pallas_call(
         finish,

time: 59.1 us -> 53.6 us (0.907)
  Pallas kernels: 56.9 us -> 52.8 us
  local copies, waits for them, and re-layouts: 1.36 us -> 0 us
    pallas_call x1, Pallas kernels: 52.7 us -> 49.4 us  [on_device(): pl.pallas_call(kernel, out_shape=(jax.ShapeDtypeStruct((classes, points),...]
    unnamed x1 -> x0, local copies, waits for them, and re-layouts: 1.36 us -> none
    pallas_call x1, Pallas kernels: 4.21 us -> 3.41 us  [on_device(): pl.pallas_call(finish, grid=(points // FINISH,), out_shape=[jax.ShapeDtyp...]
where the time goes in v3:
time: 53.6 us; the launch traced here: 53.5 us
  Pallas kernels  52.8 us (99%)
  between operations  0.64 us (1%)
    pallas_call x1, Pallas kernels, on_device(): pl.pallas_call(kernel, out_shape=(jax.ShapeDtypeStruct((classes, points),...  49.4 us
    pallas_call x1, Pallas kernels, on_device(): pl.pallas_call(finish, grid=(points // FINISH,), out_shape=[jax.ShapeDtyp...  3.41 us

profile of v3, /device:TPU:1, one launch (start us, length us, event | category | flops | bytes accessed | tf_op | source)
XLA Modules:
  0.0 53.5 jit_solution(11262239732428876931)
XLA Ops:
  0.6 49.4 %cg_step.1 = (f32[64,4096]{1,0:T(8,128)}, f32[2,64,128]{2,1,0:T(8,128)}) custom-call(s32[8,16]{1,0:T(8,128)} %bitcast.1, s32[1,128]{1,0:T(1,128)} %base_ref.1, s32[1,8,128]{2,1,0:T(8,128)} %upper_ref.1, f32[8,4096]{1,0:T(8,128)} %feat_ref.1, f32[64,4096]{1,0:T(8,128)} %dir_ref.1, f32[64,4096]{1,0:T(8,128)} %res_any.1, f32[128,4096]{1,0:T(8,128)} %basis_any.1, ...), custom_call_target="tpu_custom_call" | custom-call | tf_op jit(solution)/shard_map/cg_step/pallas_call | solution.py:476
  50.1 3.4 %cg_finish.1 = (f32[64,4096]{1,0:T(8,128)}, f32[64,4096]{1,0:T(8,128)}, f32[64,4096]{1,0:T(8,128)}) custom-call(f32[2,64,128]{2,1,0:T(8,128)} %get-tuple-element.5.factors, f32[64,4096]{1,0:T(8,128)} %sol_ref.1, f32[64,4096]{1,0:T(8,128)} %get-tuple-element.6.nr_ref, f32[64,4096]{1,0:T(8,128)} %dir_ref.1), custom_call_target="tpu_custom_call" | custom-call | tf_op jit(solution)/shard_map/cg_finish/pallas_call | solution.py:528

commit v4 on v3

--- a/solution.py
+++ b/solution.py
@@ -28,9 +28,15 @@
 FAR_FIRST = (8, 7, 9, 6, 10, 5, 11, 4, 12, 3, 13, 2, 14, 1, 15)
 MESSAGES = sum(len(stage) for stage in STAGES)
 TEAM = 4
-TILES = INNER + 1
-STEPS = LEAVES // TEAM * TILES // 2
-SHARE = (0, 5, 4, 5, 0)
+OWN_STEPS = LEAVES // TEAM // 2
+PAIRS = LEAVES * INNER // 2
+PAIR_STEPS = PAIRS // TEAM // 2
+NOTHING = PAIRS
+UPPER = 64
+AFTER = UPPER + PAIRS
+BEFORE = AFTER + BOUND
+PLACES = BEFORE + BOUND
+SHARE = (0, 2, 2, 2, 0)
 
 
 def flip(me, mask):
@@ -101,10 +107,11 @@
 
 
 def kernel(
-    nbr_any, base_ref, upper_ref, feat_ref, dir_any, res_any, basis_any, trans_any,
-    nr_ref, ab_ref,
+    nbr_any, base_any, upper_any, feat_any, dir_any, res_any, basis_any, trans_any,
+    nr_any, ab_ref,
+    nbr_v, base_ref, upper_ref, feat_ref, nr_v,
     dir_v, res_v, basis_v, trans_v, basis_h, basis_l, trans_h, trans_l, hots,
-    source_v, target_v, value_v, near_v, edge_v, tile_v, nbr, pos_s,
+    source_v, target_v, value_v, near_v, product_v, tile_v, table_v, nbr, table_s, pos_s,
     node_v, descent_v, tree_out, tree_in, halo_out, halo_in, lo_out, lo_in, hi_out, hi_in,
     local_sem, tree_s, tree_r, halo_s, halo_r, lo_s, lo_r, hi_s, hi_r,
 ):
@@ -113,10 +120,25 @@
     hi_id = me // GROUP
     halves = [me // 2**level % 2 for level in range(LEVELS)]
 
+    barrier = pltpu.get_barrier_semaphore()
+    right = (me + 1) % 256
+    left = (me + 255) % 256
+    peers = [right, left]
+    peers += [hi_id * GROUP + (lo_id + m) % GROUP for m in range(1, GROUP)]
+    peers += [(me + GROUP * m) % 256 for m in range(1, GROUP)]
+    for peer in peers:
+        pl.semaphore_signal(barrier, inc=1, device_id=(peer,), device_id_type=MESH)
+
     copies = {}
     copies["nbr"] = pltpu.make_async_copy(nbr_any, nbr, local_sem.at[7])
     copies["nbr"].start()
     quarter = basis_v.shape[1] // 4
+    for at, (name, source, into) in enumerate((
+        ("feat", feat_any, feat_ref), ("base", base_any, base_ref),
+        ("upper", upper_any, upper_ref), ("nbr_v", nbr_any, nbr_v),
+    )):
+        copies[name] = pltpu.make_async_copy(source, into, local_sem.at[8 + at])
+        copies[name].start()
     copies["dir"] = pltpu.make_async_copy(dir_any, dir_v, local_sem.at[0])
     copies["dir"].start()
     for i in range(4):
@@ -128,15 +150,6 @@
     copies["res"] = pltpu.make_async_copy(res_any, res_v, local_sem.at[6])
     copies["res"].start()
 
-    barrier = pltpu.get_barrier_semaphore()
-    right = (me + 1) % 256
-    left = (me + 255) % 256
-    peers = [right, left]
-    peers += [hi_id * GROUP + (lo_id + m) % GROUP for m in range(1, GROUP)]
-    peers += [(me + GROUP * m) % 256 for m in range(1, GROUP)]
-    for peer in peers:
-        pl.semaphore_signal(barrier, inc=1, device_id=(peer,), device_id_type=MESH)
-
     copies["nbr"].wait()
     edges = []
     for slot in (6, 7):
@@ -146,8 +159,8 @@
         for k in range(LEAVES):
             partner = nbr[slot, k]
             filled = partner >= 0
-            place = jnp.minimum(count, BOUND - 1) + (BOUND + 1 if slot == 6 else 0)
-            pos_s[slot - 6, k] = jnp.where(filled, place, BOUND)
+            place = jnp.minimum(count, BOUND - 1) + (BEFORE if slot == 6 else AFTER)
+            pos_s[slot - 6, k] = jnp.where(filled, place, NOTHING)
             for q in range(BOUND):
                 here = filled & (count == q)
                 mine[q] = jnp.where(here, k, mine[q])
@@ -163,6 +176,8 @@
         edges.append((mine, ranks))
 
     points = jnp.zeros((32, RANK), f32)
+    copies["feat"].wait()
+    copies["base"].wait()
     base_row = base_ref[...]
     for c in range(feat_ref.shape[1] // CHUNK):
         feat = feat_ref[:, c * CHUNK : (c + 1) * CHUNK]
@@ -199,40 +214,86 @@
     def tile(source, k):
         return jnp.exp(dot(source, target_v[k])).astype(bf16)
 
-    def near_place(batch, member):
-        slot = batch % TILES
-        k = batch // TILES * TEAM + member
-        partner = nbr[jnp.maximum(slot - 1, 0), k]
-        j = jnp.where(slot == 0, k, jnp.clip(partner - me * LEAVES, 0, LEAVES - 1))
-        scale = jnp.where(slot == 0, 1.0, jnp.where(partner >= 0, 0.125, 0.0)).astype(f32)
-        return k, j, scale
-
-    def near_add(batch, buffer):
+    def own_add(batch, buffer, *members):
+        for member in members or range(TEAM):
+            k = batch * TEAM + member
+            near_v[k] = dot(value_v[k, :CLASSES, :], tile_v[buffer, member])
+
+    def own_batch(batch, buffer):
         for member in range(TEAM):
-            k, j, scale = near_place(batch, member)
-            near_v[k] = near_v[k] + scale * dot(value_v[j, :CLASSES, :], tile_v[buffer, member])
-
-    def near_batch(batch, buffer):
-        near_add(jnp.maximum(batch - 1, 0), 1 - buffer)
+            k = batch * TEAM + member
+            tile_v[buffer, member] = tile(source_v[k], k)
+        own_add(jnp.maximum(batch - 1, 0), 1 - buffer)
+
+    def own_step(step, carry):
+        own_batch(2 * step, 0)
+        own_batch(2 * step + 1, 1)
+        return carry
+
+    def leaf_of(row, p):
+        return jnp.clip(table_s[row, p], 0, LEAVES - 1)
+
+    def pair_add(batch, buffer, *members):
+        for member in members or range(TEAM):
+            p = batch * TEAM + member
+            block = tile_v[buffer, member]
+            product_v[p] = dot(value_v[leaf_of(1, p), :CLASSES, :], block)
+            product_v[UPPER + p] = dot(value_v[leaf_of(0, p), :CLASSES, :], block, NT)
+
+    def pair_batch(batch, buffer):
         for member in range(TEAM):
-            k, j, _ = near_place(batch, member)
-            tile_v[buffer, member] = tile(source_v[j], k)
-
-    def near_step(step, carry):
-        near_batch(2 * step, 0)
-        near_batch(2 * step + 1, 1)
+            p = batch * TEAM + member
+            tile_v[buffer, member] = tile(source_v[leaf_of(1, p)], leaf_of(0, p))
+            pair_add(jnp.maximum(batch - 1, 0), 1 - buffer, member)
+
+    def pair_step(step, carry):
+        pair_batch(2 * step, 0)
+        pair_batch(2 * step + 1, 1)
         return carry
 
+    def list_pairs():
+        square = (RANK, RANK)
+        lane = lax.broadcasted_iota(jnp.int32, square, 1)
+        sub = lax.broadcasted_iota(jnp.int32, square, 0)
+        local = nbr_v[...] - me * LEAVES
+        local = jnp.where((nbr_v[...] >= 0) & (local >= 0) & (local < LEAVES), local, -1)
+        copies_of = jnp.where(lane[:LEAVES] % LEAVES == sub[:LEAVES], 1.0, 0.0).astype(bf16)
+        spread_out = dot(local.astype(f32).astype(bf16), copies_of)
+        mine = (lane[:8] // LEAVES == sub[:8]) & (sub[:8] < INNER)
+        partner = jnp.sum(jnp.where(mine, spread_out, 0.0), axis=0, keepdims=True)
+        partner = jnp.where(lane[:1] < INNER * LEAVES, partner, -1.0)
+        partner_lane = jnp.broadcast_to(partner, square)
+        partner_sub = partner_lane.T
+        leaf_lane = (lane % LEAVES).astype(f32)
+        leaf_sub = (sub % LEAVES).astype(f32)
+        first_lane = partner_lane > leaf_lane
+        first_sub = partner_sub > leaf_sub
+        rank = jnp.sum(jnp.where(first_sub & (sub < lane), 1.0, 0.0), axis=0, keepdims=True)
+        rank_sub = jnp.broadcast_to(rank, square).T
+        here = first_sub & (rank_sub == lane.astype(f32))
+        lower = jnp.sum(jnp.where(here, leaf_sub, 0.0), axis=0, keepdims=True)
+        upper = jnp.sum(jnp.where(here, partner_sub, 0.0), axis=0, keepdims=True)
+        met = first_sub & (leaf_sub == partner_lane) & (partner_sub == leaf_lane)
+        back = jnp.max(jnp.where(met, rank_sub, 0.0), axis=0, keepdims=True)
+        place = jnp.where(first_lane[:1], rank, jnp.where(partner >= 0.0, UPPER + back, float(NOTHING)))
+        place = jnp.clip(place, 0.0, float(AFTER - 1))
+        table_v[0:1] = lower.astype(jnp.int32)
+        table_v[1:2] = upper.astype(jnp.int32)
+        table_v[2:3] = place.astype(jnp.int32)
+        move = pltpu.make_async_copy(table_v, table_s, local_sem.at[7])
+        move.start()
+        return move
+
     def near_edges():
-        for side, at in ((1, 0), (0, 5)):
+        for side, at in ((1, AFTER), (0, BEFORE)):
             mine, ranks = edges[side]
             for q in range(BOUND):
                 source = halo_in[side, ranks[q], CLASSES:].astype(f32).T.astype(bf16)
                 tile_v[side, q] = tile(source, mine[q])
-        for side, at in ((1, 0), (0, 5)):
+        for side, at in ((1, AFTER), (0, BEFORE)):
             ranks = edges[side][1]
             for q in range(BOUND):
-                edge_v[at + q] = 0.125 * dot(halo_in[side, ranks[q], :CLASSES], tile_v[side, q])
+                product_v[at + q] = dot(halo_in[side, ranks[q], :CLASSES], tile_v[side, q])
 
     def lane_sums(x):
         out = x[:, :RANK]
@@ -335,7 +396,10 @@
             curve, norm = carry
             cols = pl.ds(pl.multiple_of(k * WIDTH, WIDTH), WIDTH)
             d = dir_v[:, cols]
-            near = d + (near_v[k] + (edge_v[pos_s[0, k]] + edge_v[pos_s[1, k]]))
+            sides = product_v[pos_s[0, k]] + product_v[pos_s[1, k]]
+            for s in range(INNER):
+                sides = sides + product_v[jnp.clip(table_s[2, s * LEAVES + k], 0, AFTER - 1)]
+            near = d + (near_v[k] + 0.125 * sides)
             near_v[k] = near
             r = res_v[:, cols]
             return curve + lane_sums(d * near), norm + lane_sums(r * r)
@@ -350,6 +414,7 @@
     node = (weights, points)
     keep(0, node)
     copies["trans"].wait()
+    copies["upper"].wait()
     split_level(0)
     for stage, masks in enumerate(STAGES):
         gift = raised(level, halves[level], node)
@@ -369,31 +434,37 @@
         if stage == 0:
             for i in range(1, LEVELS):
                 split_level(i)
-            near_v[...] = jnp.zeros_like(near_v)
+            copies["nbr_v"].wait()
+            table_move = list_pairs()
             tile_v[1] = jnp.zeros((TEAM, WIDTH, WIDTH), bf16)
         if stage == 2:
             halo_copies = halo_start()
         if SHARE[stage]:
-            lax.fori_loop(done, done + SHARE[stage], near_step, 0)
+            if done == 0:
+                matrix, quad = coupled(0, None)
+                lax.fori_loop(0, OWN_STEPS, own_step, 0)
+                own_add(2 * OWN_STEPS - 1, 1)
+                table_move.wait()
+            lax.fori_loop(done, done + SHARE[stage], pair_step, 0)
             done += SHARE[stage]
-            if done == STEPS:
-                near_add(2 * STEPS - 1, 1)
+            for i in range(max(1, 2 * stage - 2), min(5, 2 * stage)):
+                matrix, more = coupled(i, matrix)
+                quad = quad + 0.5**i * more
+            if done == PAIR_STEPS:
+                pair_add(2 * PAIR_STEPS - 1, 1)
         if stage == 3:
             halo_copies[0].wait_recv()
             halo_copies[1].wait_recv()
-            edge_v[BOUND] = jnp.zeros((CLASSES, WIDTH), f32)
+            product_v[NOTHING] = jnp.zeros((CLASSES, WIDTH), f32)
             near_edges()
             copies["res"].wait()
             curve, norm = finish_near()
-            matrix, quad = coupled(0, None)
-            for i in range(1, 5):
-                matrix, more = coupled(i, matrix)
-                quad = quad + 0.5**i * more
             lo_first = spread(as_row(curve + quad, norm), lo_out, lo_in, lo_s, lo_r, 0, lo_id, lo_peer)
         if stage == 4:
             matrix, quad = coupled(5, matrix)
             matrix, more = coupled(6, matrix)
-            quad = 0.5 * quad + 0.25 * more
+            row = total(lo_first, lo_in, 0) + as_row(0.5 * quad + 0.25 * more, jnp.zeros_like(quad))
+            hi_first = spread(row, hi_out, hi_in, hi_s, hi_r, 0, hi_id, hi_peer)
         given = []
         for message, at in messages:
             message.wait_recv()
@@ -408,11 +479,10 @@
             level += 1
             keep(level, node)
 
-    matrix, more = coupled(7, matrix)
-    row = total(lo_first, lo_in, 0) + as_row(quad + 0.125 * more, jnp.zeros_like(quad))
-    hi_first = spread(row, hi_out, hi_in, hi_s, hi_r, 0, hi_id, hi_peer)
-    _, top = coupled(8, matrix)
-    top = as_row(top, jnp.zeros_like(top))
+    matrix, top = coupled(7, matrix)
+    top = top + other[0] * dot3(split2(other[0]), split2(gaussian(other[1])))
+    _, more = coupled(8, matrix)
+    top = as_row(top + more, jnp.zeros_like(top))
     descent = lax.fori_loop(1, LEVELS + 1, lambda i, total: total + descent_v[i], descent_v[0])
     dh, dl = split2(descent)
     both = jnp.concatenate([dh, dl], axis=0)
@@ -434,12 +504,14 @@
     def update(k, norm):
         cols = pl.ds(pl.multiple_of(k * WIDTH, WIDTH), WIDTH)
         new = res_v[:, cols] - wide_step * near_v[k]
-        nr_ref[:, cols] = new
+        nr_v[:, cols] = new
         return norm + lane_sums(new * new)
 
     norm = lax.fori_loop(0, LEAVES, update, jnp.zeros((CLASSES, RANK), f32))
     row = as_row(norm, jnp.zeros_like(norm))
     lo_second = spread(row, lo_out, lo_in, lo_s, lo_r, 1, lo_id, lo_peer)
+    nr_copy = pltpu.make_async_copy(nr_v, nr_any, local_sem.at[12])
+    nr_copy.start()
     for message in sent + halo_copies:
         message.wait_send()
     for send, _ in lo_first + hi_first:
@@ -449,6 +521,7 @@
     for send, _ in lo_second:
         send.wait_send()
     row = total(hi_second, hi_in, 1)
+    nr_copy.wait()
     ab_ref[0] = step_size
     ab_ref[1] = as_columns(row)[:CLASSES] / norm_old
 
@@ -479,9 +552,14 @@
             jax.ShapeDtypeStruct((classes, points), f32),
             jax.ShapeDtypeStruct((2, classes, RANK), f32),
         ),
-        in_specs=[whole, vmem, vmem, vmem, whole, whole, whole, whole],
-        out_specs=(vmem, vmem),
+        in_specs=[whole] * 8,
+        out_specs=(whole, vmem),
         scratch_shapes=[
+            pltpu.VMEM((8, LEAVES), jnp.int32),
+            pltpu.VMEM((1, RANK), jnp.int32),
+            pltpu.VMEM((1, LEVELS, RANK), jnp.int32),
+            pltpu.VMEM((DIMS, points), f32),
+            pltpu.VMEM((classes, points), f32),
             pltpu.VMEM((classes, points), f32),
             pltpu.VMEM((classes, points), f32),
             pltpu.VMEM((RANK, points), f32),
@@ -495,9 +573,11 @@
             pltpu.VMEM((LEAVES, 16, WIDTH), bf16),
             pltpu.VMEM((LEAVES, CLASSES + 16, WIDTH), bf16),
             pltpu.VMEM((LEAVES, CLASSES, WIDTH), f32),
-            pltpu.VMEM((9, CLASSES, WIDTH), f32),
+            pltpu.VMEM((PLACES, CLASSES, WIDTH), f32),
             pltpu.VMEM((2, TEAM, WIDTH, WIDTH), bf16),
+            pltpu.VMEM((8, RANK), jnp.int32),
             pltpu.SMEM((8, LEAVES), jnp.int32),
+            pltpu.SMEM((8, RANK), jnp.int32),
             pltpu.SMEM((2, LEAVES), jnp.int32),
             pltpu.VMEM((LEVELS + 1, CLASSES + DIMS, RANK), f32),
             pltpu.VMEM((LEVELS + 1, CLASSES, RANK), f32),
@@ -509,7 +589,7 @@
             pltpu.VMEM((2, GROUP, 1, RANK), f32),
             pltpu.VMEM((2, 1, RANK), f32),
             pltpu.VMEM((2, GROUP, 1, RANK), f32),
-            dma((8,)),
+            dma((13,)),
             dma((MESSAGES,)),
             dma((MESSAGES,)),
             dma((2,)),

time: 53.6 us -> 52.1 us (0.972)
  Pallas kernels: 52.8 us -> 51.4 us
    pallas_call x1, Pallas kernels: 49.4 us -> 47.9 us  [on_device(): pl.pallas_call(kernel, out_shape=(jax.ShapeDtypeStruct((classes, points),...]
where the time goes in v4:
time: 52.1 us; the launch traced here: 52 us
  Pallas kernels  51.4 us (99%)
  between operations  0.64 us (1%)
    pallas_call x1, Pallas kernels, on_device(): pl.pallas_call(kernel, out_shape=(jax.ShapeDtypeStruct((classes, points),...  47.9 us
    pallas_call x1, Pallas kernels, on_device(): pl.pallas_call(finish, grid=(points // FINISH,), out_shape=[jax.ShapeDtyp...  3.48 us

profile of v4, /device:TPU:1, one launch (start us, length us, event | category | flops | bytes accessed | tf_op | source)
XLA Modules:
  0.0 52.0 jit_solution(7150758241919567421)
XLA Ops:
  0.6 47.9 %cg_step.1 = (f32[64,4096]{1,0:T(8,128)}, f32[2,64,128]{2,1,0:T(8,128)}) custom-call(s32[8,16]{1,0:T(8,128)} %bitcast.1, s32[1,128]{1,0:T(1,128)} %base_any.1, s32[1,8,128]{2,1,0:T(8,128)} %upper_any.1, f32[8,4096]{1,0:T(8,128)} %feat_any.1, f32[64,4096]{1,0:T(8,128)} %dir_ref.1, f32[64,4096]{1,0:T(8,128)} %res_any.1, f32[128,4096]{1,0:T(8,128)} %basis_any.1, ...), custom_call_target="tpu_custom_call" | custom-call | tf_op jit(solution)/shard_map/cg_step/pallas_call | solution.py:549
  48.5 3.5 %cg_finish.1 = (f32[64,4096]{1,0:T(8,128)}, f32[64,4096]{1,0:T(8,128)}, f32[64,4096]{1,0:T(8,128)}) custom-call(f32[2,64,128]{2,1,0:T(8,128)} %get-tuple-element.5.factors, f32[64,4096]{1,0:T(8,128)} %sol_ref.1, f32[64,4096]{1,0:T(8,128)} %get-tuple-element.6.nr_ref, f32[64,4096]{1,0:T(8,128)} %dir_ref.1), custom_call_target="tpu_custom_call" | custom-call | tf_op jit(solution)/shard_map/cg_finish/pallas_call | solution.py:608

commit v5 on v4

--- a/solution.py
+++ b/solution.py
@@ -437,7 +437,7 @@
             copies["nbr_v"].wait()
             table_move = list_pairs()
             tile_v[1] = jnp.zeros((TEAM, WIDTH, WIDTH), bf16)
-        if stage == 2:
+        if stage == 1:
             halo_copies = halo_start()
         if SHARE[stage]:
             if done == 0:

time: 52.1 us -> 50.5 us (0.969)
  Pallas kernels: 51.4 us -> 49.7 us
    pallas_call x1, Pallas kernels: 47.9 us -> 46.2 us  [on_device(): pl.pallas_call(kernel, out_shape=(jax.ShapeDtypeStruct((classes, points),...]
where the time goes in v5:
time: 50.5 us; the launch traced here: 50.3 us
  Pallas kernels  49.7 us (98%)
  between operations  0.64 us (1%)
    pallas_call x1, Pallas kernels, on_device(): pl.pallas_call(kernel, out_shape=(jax.ShapeDtypeStruct((classes, points),...  46.2 us
    pallas_call x1, Pallas kernels, on_device(): pl.pallas_call(finish, grid=(points // FINISH,), out_shape=[jax.ShapeDtyp...  3.48 us

profile of v5, /device:TPU:1, one launch (start us, length us, event | category | flops | bytes accessed | tf_op | source)
XLA Modules:
  0.0 50.3 jit_solution(16224833997608882058)
XLA Ops:
  0.6 46.2 %cg_step.1 = (f32[64,4096]{1,0:T(8,128)}, f32[2,64,128]{2,1,0:T(8,128)}) custom-call(s32[8,16]{1,0:T(8,128)} %bitcast.1, s32[1,128]{1,0:T(1,128)} %base_any.1, s32[1,8,128]{2,1,0:T(8,128)} %upper_any.1, f32[8,4096]{1,0:T(8,128)} %feat_any.1, f32[64,4096]{1,0:T(8,128)} %dir_ref.1, f32[64,4096]{1,0:T(8,128)} %res_any.1, f32[128,4096]{1,0:T(8,128)} %basis_any.1, ...), custom_call_target="tpu_custom_call" | custom-call | tf_op jit(solution)/shard_map/cg_step/pallas_call | solution.py:549
  46.9 3.5 %cg_finish.1 = (f32[64,4096]{1,0:T(8,128)}, f32[64,4096]{1,0:T(8,128)}, f32[64,4096]{1,0:T(8,128)}) custom-call(f32[2,64,128]{2,1,0:T(8,128)} %get-tuple-element.5.factors, f32[64,4096]{1,0:T(8,128)} %sol_ref.1, f32[64,4096]{1,0:T(8,128)} %get-tuple-element.6.nr_ref, f32[64,4096]{1,0:T(8,128)} %dir_ref.1), custom_call_target="tpu_custom_call" | custom-call | tf_op jit(solution)/shard_map/cg_finish/pallas_call | solution.py:608
